TPU v7x, 128 devices: a whole 4x4x4 slice. The times are simulated.
128 devices in a mesh: dp: 32 (over x, y, core), seq: 4 (over z).
Axes of the slice: x: 4, y: 4, z: 4, core: 2. Of those that a mesh axis runs over, the one named last changes fastest.
Arguments:
- hidden_in: bfloat16 [2, 32, 1024, 1024], P(None, 'dp', 'seq'), may hold values from -6 to 6
- segments: int32 [2, 32, 1024], P(None, 'dp'), may hold values from 0 to 1023, as said below
- valid_mask: int32 [2, 32, 1024], P(None, 'dp'), may hold values from 0 to 1, as said below
- w_qkv: bfloat16 [1024, 3072], P(('dp', 'seq')), may hold values from -0.1875 to 0.1875
- w_out: bfloat16 [1024, 1024], P(('dp', 'seq')), may hold values from -1.5 to 1.5
- w_up: bfloat16 [1024, 4096], P(('dp', 'seq')), may hold values from -0.1875 to 0.1875
- w_down: bfloat16 [4096, 1024], P(('dp', 'seq')), may hold values from -0.09375 to 0.09375
- b_qkv: bfloat16 [3072], P(('dp', 'seq')), may hold values from -3 to 3
- b_out: bfloat16 [1024], P(('dp', 'seq')), may hold values from -3 to 3
- b_up: bfloat16 [4096], P(('dp', 'seq')), may hold values from -3 to 3
- b_down: bfloat16 [1024], P(('dp', 'seq')), may hold values from -3 to 3
- ln_gain: bfloat16 [1024], P(('dp', 'seq')), may hold values from 0.099609375 to 1.8984375
- ln_shift: bfloat16 [1024], P(('dp', 'seq')), may hold values from -3 to 3
- cotangent: bfloat16 [2, 32, 1024, 1024], P(None, 'dp', 'seq'), may hold values from -6 to 6
Outputs:
- out_hidden: bfloat16 [2, 32, 1024, 1024], P(None, 'dp', 'seq')
- grad_input: float32 [2, 32, 1024, 1024], P(None, 'dp', 'seq')
- grad_qkv: float32 [1024, 3072], P(('dp', 'seq'))
- grad_out: float32 [1024, 1024], P(('dp', 'seq'))
- grad_up: float32 [1024, 4096], P(('dp', 'seq'))
- grad_down: float32 [4096, 1024], P(('dp', 'seq'))
- grad_bqkv: float32 [3072], P(('dp', 'seq'))
- grad_bout: float32 [1024], P(('dp', 'seq'))
- grad_bup: float32 [4096], P(('dp', 'seq'))
- grad_bdown: float32 [1024], P(('dp', 'seq'))
- grad_gain: float32 [1024], P(('dp', 'seq'))
- grad_shift: float32 [1024], P(('dp', 'seq'))
Inputs may be any that keep to these rules, and one draw needn't show every extreme that they name: `segments`: along a row, segment ids start at 0 and never fall; tokens of one document are contiguous; the padding tokens form the last segment, with id 1024 - 1. `valid_mask`: along a row the ones come first and at least one zero ends it.
All inputs are finite; a program needn't handle non-finite values.
Results may differ from a plain program's by a relative error of at most 0.011.
Values may be sent and summed in bfloat16 or wider, within the bound.
No kernel may reach another device: no remote copies, remote signals or barrier semaphores. Data moves between devices by JAX's collectives and lax.ppermute only.
A program may use at most 256 MiB of HBM per device.

v0:
```python
import jax
import jax.numpy as jnp
from jax import lax
from jax.sharding import PartitionSpec as P

HEAD_DIM = 64
ROT = 32


def layer_norm(inputs, gain, shift):
    average = jnp.mean(inputs, axis=-1, keepdims=True)
    centered = inputs - average
    spread = jnp.mean(centered * centered, axis=-1, keepdims=True)
    return centered * lax.rsqrt(spread + 1e-05) * gain + shift


def doc_positions(seg_row):
    length = seg_row.shape[-1]
    token_index = jnp.arange(length, dtype=jnp.int32)
    previous = jnp.concatenate([seg_row[..., :1], seg_row[..., :-1]], axis=-1)
    starts = jnp.where((token_index == 0) | (seg_row != previous), token_index, 0)
    doc_start = lax.cummax(starts, axis=seg_row.ndim - 1)
    return token_index - doc_start


def rotary_tables(positions):
    half_dim = ROT // 2
    frequency = 10000.0 ** (-jnp.arange(half_dim, dtype=jnp.float32) * 2.0 / ROT)
    angles = positions.astype(jnp.float32)[..., None] * frequency
    return (jnp.cos(angles), jnp.sin(angles))


def rotate(tensor, cosine, sine_tab):
    half_dim = cosine.shape[-1]
    cos_b = cosine[..., None, :]
    sin_b = sine_tab[..., None, :]
    first_half = tensor[..., :half_dim]
    second = tensor[..., half_dim : 2 * half_dim]
    passed = tensor[..., 2 * half_dim :]
    return jnp.concatenate(
        [first_half * cos_b - second * sin_b, second * cos_b + first_half * sin_b, passed], axis=-1
    )


def allowed_keys(seg_query, seg_key, query_index, key_index, valid_key):
    same_doc = seg_query[:, None] == seg_key[None, :]
    causal = key_index[None, :] <= query_index[:, None]
    visible = (valid_key[None, :] > 0) | (key_index[None, :] == query_index[:, None])
    return same_doc & causal & visible


def gelu_tanh(values_in):
    return jax.nn.gelu(values_in, approximate=True)


def body(
    hidden_in,
    segments,
    valid_mask,
    w_qkv,
    w_out,
    w_up,
    w_down,
    b_qkv,
    b_out,
    b_up,
    b_down,
    ln_gain,
    ln_shift,
    cotangent,
):
    weights = (
        lax.all_gather(w_qkv, ("dp", "seq"), axis=0, tiled=True),
        lax.all_gather(w_out, ("dp", "seq"), axis=0, tiled=True),
        lax.all_gather(w_up, ("dp", "seq"), axis=0, tiled=True),
        lax.all_gather(w_down, ("dp", "seq"), axis=0, tiled=True),
        lax.all_gather(b_qkv, ("dp", "seq"), axis=0, tiled=True),
        lax.all_gather(b_out, ("dp", "seq"), axis=0, tiled=True),
        lax.all_gather(b_up, ("dp", "seq"), axis=0, tiled=True),
        lax.all_gather(b_down, ("dp", "seq"), axis=0, tiled=True),
        lax.all_gather(ln_gain, ("dp", "seq"), axis=0, tiled=True),
        lax.all_gather(ln_shift, ("dp", "seq"), axis=0, tiled=True),
    )
    micro_count = hidden_in.shape[0]
    group_len = hidden_in.shape[2]
    model_width = hidden_in.shape[3]
    head_count = model_width // HEAD_DIM
    row_len = group_len * lax.axis_size("seq")
    offset = lax.axis_index("seq") * group_len
    score_scale = HEAD_DIM ** (-0.5)
    inputs_f = hidden_in[:, 0].astype(jnp.float32)
    seg_rows = segments[:, 0]
    valid_rows = valid_mask[:, 0]
    gain_f = weights[8].astype(jnp.float32)
    shift_f = weights[9].astype(jnp.float32)
    normed_r = layer_norm(inputs_f, gain_f, shift_f).astype(jnp.bfloat16)
    qkv_f = jnp.dot(normed_r, weights[0], preferred_element_type=jnp.float32) + weights[4].astype(
        jnp.float32
    )
    positions = lax.dynamic_slice_in_dim(doc_positions(seg_rows), offset, group_len, 1)
    cosine, sine_tab = rotary_tables(positions)

    def rotate_local(tensor):
        return rotate(tensor, cosine, sine_tab)

    split_shape = (micro_count, group_len, head_count, HEAD_DIM)
    raw_q = qkv_f[..., :model_width].reshape(split_shape)
    raw_k = qkv_f[..., model_width : 2 * model_width].reshape(split_shape)
    queries_r = rotate_local(raw_q).astype(jnp.bfloat16)
    keys_r = rotate_local(raw_k).astype(jnp.bfloat16).reshape(micro_count, group_len, model_width)
    values_r = qkv_f[..., 2 * model_width :].astype(jnp.bfloat16)
    all_keys, all_values = (
        lax.all_gather(keys_r, "seq", axis=1, tiled=True),
        lax.all_gather(values_r, "seq", axis=1, tiled=True),
    )
    key_index = jnp.arange(row_len, dtype=jnp.int32)
    query_index = offset + jnp.arange(group_len, dtype=jnp.int32)
    key_masks = []
    mixed_parts = []
    lse_parts = []
    for micro_idx in range(micro_count):
        seg_query = lax.dynamic_slice_in_dim(seg_rows[micro_idx], offset, group_len, 0)
        allowed = allowed_keys(
            seg_query, seg_rows[micro_idx], query_index, key_index, valid_rows[micro_idx]
        )
        key_heads = all_keys[micro_idx].reshape(row_len, head_count, HEAD_DIM)
        value_heads = all_values[micro_idx].reshape(row_len, head_count, HEAD_DIM)
        scores = (
            jnp.einsum(
                "qhd,khd->hqk", queries_r[micro_idx], key_heads, preferred_element_type=jnp.float32
            )
            * score_scale
        )
        masked = jnp.where(allowed[None], scores, -1e30)
        row_max = jnp.max(masked, axis=-1, keepdims=True)
        exponent = jnp.exp(masked - row_max)
        row_total = jnp.sum(exponent, axis=-1, keepdims=True)
        probs_r = (exponent / row_total).astype(jnp.bfloat16)
        mixed_parts.append(
            jnp.einsum(
                "hqk,khd->qhd", probs_r, value_heads, preferred_element_type=jnp.float32
            ).reshape(group_len, model_width)
        )
        lse_parts.append(row_max + jnp.log(row_total))
        key_masks.append(allowed)
    mixed_r = jnp.stack(mixed_parts).astype(jnp.bfloat16)
    attn_branch = jnp.dot(mixed_r, weights[1], preferred_element_type=jnp.float32) + weights[
        5
    ].astype(jnp.float32)
    up_f = jnp.dot(normed_r, weights[2], preferred_element_type=jnp.float32) + weights[6].astype(
        jnp.float32
    )
    act_r = gelu_tanh(up_f).astype(jnp.bfloat16)
    mlp_branch = jnp.dot(act_r, weights[3], preferred_element_type=jnp.float32) + weights[7].astype(
        jnp.float32
    )
    out_hidden = (inputs_f + attn_branch + mlp_branch).astype(jnp.bfloat16)[:, None]
    back_weights = (
        lax.all_gather(w_qkv, ("dp", "seq"), axis=0, tiled=True),
        lax.all_gather(w_out, ("dp", "seq"), axis=0, tiled=True),
        lax.all_gather(w_up, ("dp", "seq"), axis=0, tiled=True),
        lax.all_gather(w_down, ("dp", "seq"), axis=0, tiled=True),
        lax.all_gather(b_qkv, ("dp", "seq"), axis=0, tiled=True),
        lax.all_gather(b_out, ("dp", "seq"), axis=0, tiled=True),
        lax.all_gather(b_up, ("dp", "seq"), axis=0, tiled=True),
        lax.all_gather(b_down, ("dp", "seq"), axis=0, tiled=True),
        lax.all_gather(ln_gain, ("dp", "seq"), axis=0, tiled=True),
        lax.all_gather(ln_shift, ("dp", "seq"), axis=0, tiled=True),
    )
    cot_r = cotangent[:, 0]
    cot_f = cot_r.astype(jnp.float32)
    grad_out = jnp.einsum("mci,mcj->ij", mixed_r, cot_r, preferred_element_type=jnp.float32)
    grad_bout = jnp.sum(cot_f, axis=(0, 1))
    grad_down = jnp.einsum("mci,mcj->ij", act_r, cot_r, preferred_element_type=jnp.float32)
    grad_bdown = jnp.sum(cot_f, axis=(0, 1))
    d_mixed = jnp.einsum(
        "mcj,ij->mci", cot_r, back_weights[1], preferred_element_type=jnp.float32
    ).astype(jnp.bfloat16)
    d_act = jnp.einsum("mcj,ij->mci", cot_r, back_weights[3], preferred_element_type=jnp.float32)
    _, gelu_pull = jax.vjp(gelu_tanh, up_f)
    d_up_r = gelu_pull(d_act)[0].astype(jnp.bfloat16)
    grad_up = jnp.einsum("mci,mcj->ij", normed_r, d_up_r, preferred_element_type=jnp.float32)
    grad_bup = jnp.sum(d_up_r.astype(jnp.float32), axis=(0, 1))
    dq_parts = []
    dk_parts = []
    dv_parts = []
    for micro_idx in range(micro_count):
        key_heads = all_keys[micro_idx].reshape(row_len, head_count, HEAD_DIM)
        value_heads = all_values[micro_idx].reshape(row_len, head_count, HEAD_DIM)
        query_heads = queries_r[micro_idx]
        scores = (
            jnp.einsum("qhd,khd->hqk", query_heads, key_heads, preferred_element_type=jnp.float32)
            * score_scale
        )
        masked = jnp.where(key_masks[micro_idx][None], scores, -1e30)
        probs_f = jnp.exp(masked - lse_parts[micro_idx])
        probs_r = probs_f.astype(jnp.bfloat16)
        d_heads = d_mixed[micro_idx].reshape(group_len, head_count, HEAD_DIM)
        d_probs = jnp.einsum(
            "qhd,khd->hqk", d_heads, value_heads, preferred_element_type=jnp.float32
        )
        d_total = jnp.sum(probs_f * d_probs, axis=-1, keepdims=True)
        d_scores = (probs_f * (d_probs - d_total)).astype(jnp.bfloat16)
        dq_parts.append(
            jnp.einsum("hqk,khd->qhd", d_scores, key_heads, preferred_element_type=jnp.float32)
            * score_scale
        )
        dk_parts.append(
            (
                jnp.einsum(
                    "hqk,qhd->khd", d_scores, query_heads, preferred_element_type=jnp.float32
                )
                * score_scale
            ).reshape(row_len, model_width)
        )
        dv_parts.append(
            jnp.einsum(
                "hqk,qhd->khd", probs_r, d_heads, preferred_element_type=jnp.float32
            ).reshape(row_len, model_width)
        )
    d_queries = jnp.stack(dq_parts)
    d_keys_all = jnp.stack(dk_parts)
    d_values_all = jnp.stack(dv_parts)
    d_keys, d_values = (
        lax.psum_scatter(d_keys_all, "seq", scatter_dimension=1, tiled=True),
        lax.psum_scatter(d_values_all, "seq", scatter_dimension=1, tiled=True),
    )
    _, rotate_pull = jax.vjp(rotate_local, raw_q)
    d_raw_q = rotate_pull(d_queries)[0].reshape(micro_count, group_len, model_width)
    d_raw_k = rotate_pull(d_keys.reshape(split_shape))[0].reshape(
        micro_count, group_len, model_width
    )
    d_qkv_r = jnp.concatenate([d_raw_q, d_raw_k, d_values], axis=-1).astype(jnp.bfloat16)
    grad_qkv = jnp.einsum("mci,mcj->ij", normed_r, d_qkv_r, preferred_element_type=jnp.float32)
    grad_bqkv = jnp.sum(d_qkv_r.astype(jnp.float32), axis=(0, 1))
    d_normed = jnp.einsum(
        "mcj,ij->mci", d_qkv_r, back_weights[0], preferred_element_type=jnp.float32
    )
    d_normed = d_normed + jnp.einsum(
        "mcj,ij->mci", d_up_r, back_weights[2], preferred_element_type=jnp.float32
    )
    _, norm_pull = jax.vjp(layer_norm, inputs_f, gain_f, shift_f)
    d_inputs, grad_gain, grad_shift = norm_pull(d_normed)
    grad_input = (cot_f + d_inputs)[:, None]
    summed = (
        lax.psum_scatter(grad_qkv, ("dp", "seq"), scatter_dimension=0, tiled=True),
        lax.psum_scatter(grad_out, ("dp", "seq"), scatter_dimension=0, tiled=True),
        lax.psum_scatter(grad_up, ("dp", "seq"), scatter_dimension=0, tiled=True),
        lax.psum_scatter(grad_down, ("dp", "seq"), scatter_dimension=0, tiled=True),
        lax.psum_scatter(grad_bqkv, ("dp", "seq"), scatter_dimension=0, tiled=True),
        lax.psum_scatter(grad_bout, ("dp", "seq"), scatter_dimension=0, tiled=True),
        lax.psum_scatter(grad_bup, ("dp", "seq"), scatter_dimension=0, tiled=True),
        lax.psum_scatter(grad_bdown, ("dp", "seq"), scatter_dimension=0, tiled=True),
        lax.psum_scatter(grad_gain, ("dp", "seq"), scatter_dimension=0, tiled=True),
        lax.psum_scatter(grad_shift, ("dp", "seq"), scatter_dimension=0, tiled=True),
    )
    return (
        out_hidden,
        grad_input,
        summed[0],
        summed[1],
        summed[2],
        summed[3],
        summed[4],
        summed[5],
        summed[6],
        summed[7],
        summed[8],
        summed[9],
    )


def solution(mesh):
    in_specs = (
        P(None, "dp", "seq", None),
        P(None, "dp", None),
        P(None, "dp", None),
        P(("dp", "seq"), None),
        P(("dp", "seq"), None),
        P(("dp", "seq"), None),
        P(("dp", "seq"), None),
        P(("dp", "seq")),
        P(("dp", "seq")),
        P(("dp", "seq")),
        P(("dp", "seq")),
        P(("dp", "seq")),
        P(("dp", "seq")),
        P(None, "dp", "seq", None),
    )
    out_specs = (
        P(None, "dp", "seq", None),
        P(None, "dp", "seq", None),
        P(("dp", "seq"), None),
        P(("dp", "seq"), None),
        P(("dp", "seq"), None),
        P(("dp", "seq"), None),
        P(("dp", "seq")),
        P(("dp", "seq")),
        P(("dp", "seq")),
        P(("dp", "seq")),
        P(("dp", "seq")),
        P(("dp", "seq")),
    )
    return jax.shard_map(body, mesh=mesh, in_specs=in_specs, out_specs=out_specs, check_vma=False)
```

profile of v0, /device:TPU:0, one launch (start us, length us, event | category | flops | bytes accessed | tf_op | source)
XLA Modules:
  0.0 2765.7 jit_solution(7186350106446790907)
XLA Ops:
  13.8 69.6 %all-reduce.18 = (bf16[1024]{0:T(1024)(128)(2,1)S(1)}, bf16[1024]{0:T(1024)(128)(2,1)S(1)}, bf16[4096]{0:T(1024)(128)(2,1)}, bf16[1024]{0:T(1024)(128)(2,1)}, bf...) all-reduce(bf16[1024]{0:T(1024)(128)(2,1)S(1)} %dynamic-update-slic, ...), channel_id=1, replica_groups=mesh['dp'=32,'seq'=4] {'dp','seq'}, use_global_device_ids=true, to_apply=%add.7 | all-reduce | flops 11264 | bytes 45056
  84.9 1.6 fusion.47
  87.2 6.1 fusion.33
  93.3 2.7 copy-done.14
  98.7 4.0 fusion.95
  102.7 2.9 copy.76
  105.6 2.1 slice.157
  107.7 1.8 copy.77
  110.9 1.9 subtract_convert_fusion.1
  115.4 1.6 fusion.80
  117.0 30.8 %all-gather.13.cloned.1.call-done = bf16[1024,1024]{1,0:T(8,128)(2,1)} async-done(((bf16[8,1024]{1,0:T(8,128)(2,1)}), bf16[1024,1024]{1,0:T(8,128)(2,1)}) %all-gather.13.cloned.1.call-update) | async-done | bytes 2097168 | tf_op jit(solution)/shard_map/all_gather | solution.py:74
  147.8 2.9 fusion.61
  152.7 43.2 %all-gather.9.cloned.1.call-done = bf16[2,1024,1024]{2,1,0:T(8,128)(2,1)} async-done(((bf16[2,256,1024]{2,1,0:T(8,128)(2,1)}), bf16[2,1024,1024]{2,1,0:T(8,128)(2,1)}) %all-gather.9.cloned.1.call-update) | async-done | bytes 4194320 | tf_op jit(solution)/shard_map/all_gather | solution.py:114
  196.0 4.0 fusion.97
  199.9 4.1 copy.75
  204.0 2.5 copy.78
  206.6 43.3 %all-gather.11.cloned.1.call-done = bf16[2,1024,1024]{1,2,0:T(8,128)(2,1)} async-done(((bf16[2,256,1024]{1,2,0:T(8,128)(2,1)}), bf16[2,1024,1024]{1,2,0:T(8,128)(2,1)}) %all-gather.11.cloned.1.call-update) | async-done | bytes 4194320 | tf_op jit(solution)/shard_map/all_gather | solution.py:113
  249.9 2.7 fusion.96
  252.7 3.1 fusion.100
  255.8 3.8 fusion.1
  261.0 7.4 fusion.101
  268.4 7.7 fusion
  276.8 10.6 multiply_reduce_fusion
  287.3 8.0 multiply_convert_fusion
  295.3 4.1 convolution_multiply_fusion
  299.9 15.3 multiply_reduce_fusion.1
  315.2 1.8 slice-done.2
  318.4 7.8 multiply_convert_fusion.1
  327.8 2.7 copy-done.2
  331.4 4.3 pad_maximum_fusion
  336.8 9.5 fusion.11
  346.3 5.4 copy.84
  351.7 9.7 fusion.13
  361.3 5.4 copy.83
  366.7 8.5 pad_maximum_fusion.1
  376.0 9.1 fusion.69
  386.2 8.9 fusion.70
  396.4 4.5 convolution_bitcast_fusion.3
  401.1 7.3 fusion.21
  408.4 3.3 copy-done.55
  411.6 9.7 convolution_bitcast_fusion
  421.4 13.3 convert_reduce_fusion
  434.8 2.0 copy-done.56
  436.7 8.6 convolution_bitcast_fusion.1
  445.4 6.9 fusion.64
  452.4 6.5 fusion.65
  460.0 15.3 reduce-scatter.7.cloned.1.call-done
  475.2 2.4 split.28
  477.6 2.6 multiply_add_fusion.1
  481.3 1.7 copy.85
  483.0 1.7 add_convert_fusion
  486.0 72.0 %reduce-scatter.9.cloned.1.call-done = f32[2,256,1024]{2,1,0:T(8,128)} async-done(((f32[2,1024,1024]{2,1,0:T(8,128)}), f32[2,256,1024]{2,1,0:T(8,128)}) %reduce-scatter.9.cloned.1.call-update) | async-done | bytes 2097168 | tf_op jit(solution)/shard_map/reduce_scatter | solution.py:226
  558.0 1.7 convert.55
  559.8 9.4 convolution_bitcast_fusion.2
  569.9 8.4 fusion.19
  578.3 10.8 fusion.17
  589.2 2.4 fusion.66
  591.6 3.8 fusion.94
  597.1 2.2 convert_reduce_fusion.2
  599.3 66.6 %all-reduce.17 = (f32[3072]{0:T(1024)S(1)}, f32[1024]{0:T(1024)S(1)}, f32[4096]{0:T(1024)S(1)}, f32[1024]{0:T(1024)S(1)}, f32[1024]{0:T(1024)S(1)}) all-reduce(f32[3072]{0:T(1024)S(1)} %convert_reduce_fusion.1, f32[1024]{0:T(1024)S(1)} %get-tuple-element.79, ...), channel_id=8, replica_groups=mesh['dp'=32,'seq'=4] {'dp','seq'}, use_global_device_ids=true, to_apply=%region_19.20.clone | all-reduce | flops 10240 | bytes 81920
  668.3 536.9 %reduce-scatter.13.cloned.1.call-done = f32[8,1024]{1,0:T(8,128)} async-done(((f32[1024,1024]{1,0:T(8,128)}), f32[8,1024]{1,0:T(8,128)}) %reduce-scatter.13.cloned.1.call-update) | async-done | bytes 32784 | tf_op jit(solution)/shard_map/reduce_scatter | solution.py:247
  1205.3 665.0 %reduce-scatter.17.cloned.1.call-done = f32[32,1024]{1,0:T(8,128)} async-done(((f32[4096,1024]{1,0:T(8,128)}), f32[32,1024]{1,0:T(8,128)}) %reduce-scatter.17.cloned.1.call-update) | async-done | bytes 131088 | tf_op jit(solution)/shard_map/reduce_scatter | solution.py:249
  1870.2 665.4 %reduce-scatter.15.cloned.1.call-done = f32[8,4096]{1,0:T(8,128)} async-done(((f32[1024,4096]{1,0:T(8,128)}), f32[8,4096]{1,0:T(8,128)}) %reduce-scatter.15.cloned.1.call-update) | async-done | bytes 131088 | tf_op jit(solution)/shard_map/reduce_scatter | solution.py:248
  2535.7 222.2 %reduce-scatter.11.cloned.1.call-done = f32[8,3072]{1,0:T(8,128)} async-done(((f32[1024,3072]{1,0:T(8,128)}), f32[8,3072]{1,0:T(8,128)}) %reduce-scatter.11.cloned.1.call-update) | async-done | bytes 98320 | tf_op jit(solution)/shard_map/reduce_scatter | solution.py:246
  (214 shorter events, 36.6 us)
Async XLA Ops:
  7.2 80.0 %all-gather.7.cloned.1.call-start = ((), (), s32[]{:S(2)}) async-start(), calls=%async_computation.6 | async-start | bytes 6340608 | tf_op jit(solution)/shard_map/all_gather | solution.py:73
  7.9 139.8 %all-gather.13.cloned.1.call-start = ((), (), s32[]{:S(2)}) async-start(), calls=%async_computation.9 | async-start | bytes 2113536 | tf_op jit(solution)/shard_map/all_gather | solution.py:74
  8.7 187.3 %all-gather.9.cloned.1.call-start = ((), (), s32[]{:S(2)}) async-start(), calls=%async_computation.7 | async-start | bytes 5242880 | tf_op jit(solution)/shard_map/all_gather | solution.py:114
  83.4 9.8 copy-start.30
  83.4 9.8 copy-start.28
  84.9 8.4 copy-start.32
  87.1 6.2 copy-start.36
  87.1 10.1 copy-start.42
  93.3 2.7 copy-start.14
  97.1 152.8 %all-gather.11.cloned.1.call-start = ((), (), s32[]{:S(2)}) async-start(), calls=%async_computation.8 | async-start | bytes 5242880 | tf_op jit(solution)/shard_map/all_gather | solution.py:113
  98.6 12.3 copy-start.24
  98.7 12.3 copy-start.26
  109.5 3.4 copy-start.15
  110.9 4.4 copy-start.50
  110.9 36.8 %copy-start.18 = (bf16[2,1,256,1024]{3,2,1,0:T(8,128)(2,1)S(1)}, bf16[2,1,256,1024]{3,2,1,0:T(8,128)(2,1)}, u32[]{:S(2)}) copy-start(bf16[2,1,256,1024]{3,2,1,0:T(8,128)(2,1)} %param.27) | copy-start | bytes 3145732
  114.1 286.9 %all-gather.15.cloned.1.call-start = ((), (), s32[]{:S(2)}) async-start(), calls=%async_computation.10 | async-start | bytes 8454144 | tf_op jit(solution)/shard_map/all_gather | solution.py:75
  114.7 306.7 %all-gather.17.cloned.1.call-start = ((), (), s32[]{:S(2)}) async-start(), calls=%async_computation.11 | async-start | bytes 8454144 | tf_op jit(solution)/shard_map/all_gather | solution.py:76
  115.3 360.0 %reduce-scatter.7.cloned.1.call-start = ((), (), s32[]{:S(2)}) async-start(), calls=%async_computation.12 | async-start | bytes 10485760 | tf_op jit(solution)/shard_map/reduce_scatter | solution.py:225
  249.9 2.7 copy-start.17
  252.6 3.2 copy-start.7
  252.6 8.4 copy-start.5
  255.8 3.9 copy-start.38
  255.8 31.5 %copy-start = (f32[16,256,1024]{2,1,0:T(8,128)}, f32[16,256,1024]{2,1,0:T(8,128)S(1)}, u32[]{:S(2)}) copy-start(f32[16,256,1024]{2,1,0:T(8,128)S(1)} %get-tuple-element.93) | copy-start | bytes 50331652
  255.8 5.2 copy-start.16
  268.4 7.7 copy-start.40
  295.3 4.5 copy-start.1
  299.8 15.3 slice-start
  299.8 15.4 slice-start.1
  299.8 17.1 slice-start.2
  299.8 18.5 slice-start.3
  326.2 4.3 copy-start.2
  326.2 5.2 copy-start.3
  335.7 222.3 %reduce-scatter.9.cloned.1.call-start = ((), (), s32[]{:S(2)}) async-start(), calls=%async_computation.13 | async-start | bytes 10485760 | tf_op jit(solution)/shard_map/reduce_scatter | solution.py:226
  346.3 5.4 copy-start.12
  346.3 5.4 copy-start.35
  375.2 10.9 copy-start.11
  375.2 10.9 copy-start.41
  375.2 10.9 copy-start.46
  375.2 830.0 %reduce-scatter.13.cloned.1.call-start = ((), (), s32[]{:S(2)}) async-start(), calls=%async_computation.15 | async-start | bytes 4227072 | tf_op jit(solution)/shard_map/reduce_scatter | solution.py:247
  386.2 10.1 copy-start.19
  396.3 4.6 copy-start.22
  396.3 4.7 copy-start.49
  396.3 4.7 copy-start.4
  396.3 4.7 copy-start.29
  396.3 4.7 copy-start.31
  396.4 4.7 copy-start.33
  396.4 4.7 copy-start.37
  400.9 1469.3 %reduce-scatter.17.cloned.1.call-start = ((), (), s32[]{:S(2)}) async-start(), calls=%async_computation.17 | async-start | bytes 16908288 | tf_op jit(solution)/shard_map/reduce_scatter | solution.py:249
  408.4 3.3 copy-start.55
  421.4 2114.3 %reduce-scatter.15.cloned.1.call-start = ((), (), s32[]{:S(2)}) async-start(), calls=%async_computation.16 | async-start | bytes 16908288 | tf_op jit(solution)/shard_map/reduce_scatter | solution.py:248
  434.8 2.0 copy-start.56
  445.4 7.0 copy-start.6
  445.4 2312.5 %reduce-scatter.11.cloned.1.call-start = ((), (), s32[]{:S(2)}) async-start(), calls=%async_computation.14 | async-start | bytes 12681216 | tf_op jit(solution)/shard_map/reduce_scatter | solution.py:246
  452.3 6.6 copy-start.8
  452.4 7.5 copy-start.25
  452.4 7.5 copy-start.27
  569.8 21.7 slice-start.4
  578.2 10.9 copy-start.21
  578.2 10.9 copy-start.23
  578.2 10.9 copy-start.53
  578.3 13.3 slice-start.5
  589.1 2.5 copy-start.10
  591.6 3.8 copy-start.48
  666.0 2092.4 %copy-start.54 = (f32[8]{0:T(128)}, f32[8]{0:T(128)S(1)}, u32[]{:S(2)}) copy-start(f32[8]{0:T(128)S(1)} %dynamic-slice.3) | copy-start | bytes 100
  (11 other events, 10.2 us)
Sparse Core Ops, SparseCore 0:
  11.1 71.1 all-gather.6
  85.3 62.4 all-gather.12
  150.0 45.9 all-gather.8
  197.5 52.3 all-gather.10
  252.9 70.9 all-gather.14
  326.8 67.6 all-gather.16
  397.0 78.2 reduce-scatter.6
  477.7 80.2 reduce-scatter.8
  561.0 644.2 reduce-scatter.12
  1208.2 661.9 reduce-scatter.16
  1873.3 662.2 reduce-scatter.14
  2541.8 215.9 reduce-scatter.10
where the time goes:
time: 2770 us
  waiting for transfers between devices  2300 us (83%)
  matrix products  180 us (6%)
  blocking collectives  136 us (5%)
  local copies, waits for them, and re-layouts  74.5 us (3%)
  other arithmetic  62.2 us (2%)
    reduce_scatter x1, waiting for transfers between devices, body(): lax.psum_scatter(grad_up, ('dp', 'seq'), scatter_dimension=0, tiled=True)  665 us
    reduce_scatter x1, waiting for transfers between devices, body(): lax.psum_scatter(grad_down, ('dp', 'seq'), scatter_dimension=0, tiled=True)  665 us
    reduce_scatter x1, waiting for transfers between devices, body(): lax.psum_scatter(grad_out, ('dp', 'seq'), scatter_dimension=0, tiled=True)  537 us
    reduce_scatter x1, waiting for transfers between devices, body(): lax.psum_scatter(grad_qkv, ('dp', 'seq'), scatter_dimension=0, tiled=True)  222 us
    unnamed x2, blocking collectives  136 us
    reduce_scatter x1, waiting for transfers between devices, body(): lax.psum_scatter(d_values_all, 'seq', scatter_dimension=1, tiled=True)  72 us
  transfers between devices with their start and end apart: 12, of which 9 were waited for; matrix products, arithmetic and copies ran while one was open for 11% of the time, Pallas kernels for 0%

commit v1 on v0

v1 whole, which is shorter than its diff:
```python
import jax
import jax.numpy as jnp
from jax import lax
from jax.sharding import PartitionSpec as P

HEAD_DIM = 64
ROT = 32
NZ = 4
BF = jnp.bfloat16
F32 = jnp.float32


def doc_positions(seg_row):
    length = seg_row.shape[-1]
    token_index = jnp.arange(length, dtype=jnp.int32)
    previous = jnp.concatenate([seg_row[..., :1], seg_row[..., :-1]], axis=-1)
    starts = jnp.where((token_index == 0) | (seg_row != previous), token_index, 0)
    doc_start = lax.cummax(starts, axis=seg_row.ndim - 1)
    return token_index - doc_start


def rotary_tables(positions):
    half_dim = ROT // 2
    frequency = 10000.0 ** (-jnp.arange(half_dim, dtype=F32) * 2.0 / ROT)
    angles = positions.astype(F32)[..., None] * frequency
    return (jnp.cos(angles), jnp.sin(angles))


def rotate(tensor, cosine, sine_tab):
    half_dim = cosine.shape[-1]
    cos_b = cosine[..., None, :]
    sin_b = sine_tab[..., None, :]
    first_half = tensor[..., :half_dim]
    second = tensor[..., half_dim : 2 * half_dim]
    passed = tensor[..., 2 * half_dim :]
    return jnp.concatenate(
        [first_half * cos_b - second * sin_b, second * cos_b + first_half * sin_b, passed], axis=-1
    )


def gelu_tanh(values_in):
    return jax.nn.gelu(values_in, approximate=True)


def send_z(value, step):
    return lax.ppermute(value, "seq", [(i, (i + step) % NZ) for i in range(NZ)])


def send_dp(value, dx, dy, dc):
    pairs = []
    for x in range(4):
        for y in range(4):
            for c in range(2):
                to = (((x + dx) % 4) * 4 + (y + dy) % 4) * 2 + (c + dc) % 2
                pairs.append(((x * 4 + y) * 2 + c, to))
    return lax.ppermute(value, "dp", pairs)


def gather_ring(first, second, send):
    up0, up1 = send(first, 1), send(second, 1)
    down0, down1 = send(first, -1), send(second, -1)
    far0, far1 = send(up0, 1), send(down1, -1)
    return (first, down0, far0, up0), (second, down1, far1, up1)


def reduce_ring(first, second, send):
    far0, far1 = send(first[2], 1), send(second[2], -1)

    def add(left, right):
        return (left.astype(F32) + right.astype(F32)).astype(BF)

    to_up = (add(first[1], far0), second[1])
    to_down = (first[3], add(second[3], far1))
    got_up = [send(v, 1) for v in to_up]
    got_down = [send(v, -1) for v in to_down]
    return [
        own.astype(F32) + left.astype(F32) + right.astype(F32)
        for own, left, right in zip((first[0], second[0]), got_up, got_down)
    ]


def reduce_dp(grads, place):
    x, y, c = place
    rows, cols = grads.shape[0] // 32, grads.shape[1]
    split = grads.reshape(16, 2, rows, cols)
    own = lax.dynamic_index_in_dim(split, c, 1, keepdims=False)
    other = lax.dynamic_index_in_dim(split, 1 - c, 1, keepdims=False)
    got = send_dp(other, 0, 0, 1)
    mine = (own.astype(F32) + got.astype(F32)).astype(BF).reshape(4, 4, rows, cols)
    half = cols // 2
    left, right = mine[..., :half], mine[..., half:]

    def chunks(value, at, dim):
        return [
            lax.dynamic_index_in_dim(value, (at + k) % 4, dim, keepdims=False) for k in range(4)
        ]

    def ring(value, at, dim, send):
        parts = chunks(value, at, dim)
        mid = parts[0].shape[0] // 2
        lo, hi = [p[:mid] for p in parts], [p[mid:] for p in parts]
        return jnp.concatenate(reduce_ring(lo, hi, send), axis=0)

    def along_x(value, step):
        return send_dp(value, step, 0, 0)

    def along_y(value, step):
        return send_dp(value, 0, step, 0)

    left = ring(left, x, 0, along_x).astype(BF)
    right = ring(right, y, 1, along_y).astype(BF)
    left = left.reshape(4, rows, half)
    right = right.reshape(4, rows, half)

    def ring2(value, at, send):
        parts = chunks(value, at, 0)
        mid = rows // 2
        lo, hi = [p[:mid] for p in parts], [p[mid:] for p in parts]
        return jnp.concatenate(reduce_ring(lo, hi, send), axis=0)

    left = ring2(left, y, along_y)
    right = ring2(right, x, along_x)
    return jnp.concatenate([left, right], axis=1)


def body(
    hidden_in,
    segments,
    valid_mask,
    w_qkv,
    w_out,
    w_up,
    w_down,
    b_qkv,
    b_out,
    b_up,
    b_down,
    ln_gain,
    ln_shift,
    cotangent,
):
    z = lax.axis_index("seq")
    dp = lax.axis_index("dp")
    place = (dp // 8, (dp // 2) % 4, dp % 2)
    micro_count, _, group, width = hidden_in.shape
    row_len = group * NZ
    head_count = 4

    up_cols = w_up.reshape(8, 32, 4, 32).transpose(2, 0, 1, 3).reshape(4, 8, 1024)
    qkv_cols = w_qkv.reshape(8, 3, 4, 4, 64).transpose(3, 0, 1, 2, 4).reshape(4, 8, 768)
    vectors = jnp.concatenate([b_qkv, b_out, b_up, b_down, ln_gain, ln_shift])
    vec_block = jnp.zeros((8, 128), BF).at[0, :88].set(vectors)
    outgoing = jnp.concatenate(
        [up_cols, qkv_cols, jnp.broadcast_to(vec_block, (4, 8, 128))], axis=-1
    )
    incoming = lax.all_to_all(outgoing, "seq", 0, 0, tiled=True).reshape(32, 1920)
    to_heads, from_heads = [], []
    for a in range(4):
        for zt in range(4):
            for b in range(2):
                for zs in range(4):
                    source = (8 * a + 2 * zt + b) * 4 + zs
                    target = (8 * a + 4 * b + zs) * 4 + zt
                    to_heads.append((source, target))
                    from_heads.append((target, source))
    w_out_rows = lax.ppermute(w_out, ("dp", "seq"), to_heads)
    w_out_rows = w_out_rows.reshape(8, 4, 256).transpose(1, 0, 2).reshape(32, 256)
    payload = jnp.concatenate([incoming[:, :1792], w_down, w_out_rows, incoming[:, 1792:]], axis=1)
    weights = lax.all_gather(payload, "dp", axis=0, tiled=True)

    hid = gather_ring(hidden_in[0, 0], hidden_in[1, 0], send_z)
    hidden = jnp.stack([jnp.concatenate(h, axis=0) for h in hid])
    cot = gather_ring(cotangent[0, 0], cotangent[1, 0], send_z)
    cot = jnp.stack([jnp.concatenate(h, axis=0) for h in cot])

    w_in = weights[:, :1792]
    w_dn = weights[:, 1792:2816]
    w_o = weights[:, 2816:3072].reshape(32, 4, 8, 256).transpose(0, 2, 1, 3).reshape(256, 1024)
    vecs = weights[:, 3072:].reshape(32, 4, 8, 128)[:, :, 0, :88].astype(F32)
    bq = lax.dynamic_index_in_dim(vecs[..., :24].reshape(3, 4, 4, 64), z, 2, keepdims=False)
    bq = bq.reshape(768)
    b_sum = (vecs[..., 24:32] + vecs[..., 64:72]).reshape(width)
    bu = lax.dynamic_index_in_dim(vecs[..., 32:64], z, 1, keepdims=False).reshape(1024)
    gain = vecs[..., 72:80].reshape(width)
    shift = vecs[..., 80:88].reshape(width)

    inputs_f = hidden.astype(F32)
    average = jnp.mean(inputs_f, axis=-1, keepdims=True)
    centered = inputs_f - average
    spread = jnp.mean(centered * centered, axis=-1, keepdims=True)
    rs = lax.rsqrt(spread + 1e-05)
    xhat = centered * rs
    normed = (xhat * gain + shift).astype(BF)

    both = jnp.dot(normed, w_in, preferred_element_type=F32)
    up_f = both[..., :1024] + bu
    qkv = both[..., 1024:] + bq

    order = (z * group + jnp.arange(row_len, dtype=jnp.int32)) % row_len
    seg_all = segments[:, 0]

    def turned(rows):
        return lax.dynamic_slice_in_dim(
            jnp.concatenate([rows, rows], axis=1), z * group, row_len, 1
        )

    seg = turned(seg_all)
    valid = turned(valid_mask[:, 0])
    cosine, sine_tab = rotary_tables(turned(doc_positions(seg_all)))

    def rotate_local(tensor):
        return rotate(tensor, cosine, sine_tab)

    split = (micro_count, row_len, head_count, HEAD_DIM)
    raw_q = qkv[..., :256].reshape(split)
    raw_k = qkv[..., 256:512].reshape(split)
    queries = rotate_local(raw_q).astype(BF)
    keys = rotate_local(raw_k).astype(BF)
    values = qkv[..., 512:].astype(BF).reshape(split)
    scale = HEAD_DIM ** (-0.5)

    d_mixed = jnp.einsum("mcj,ij->mci", cot, w_o, preferred_element_type=F32).astype(BF)
    d_heads = d_mixed.reshape(split)
    d_act = jnp.einsum("mcj,ij->mci", cot, w_dn, preferred_element_type=F32)
    act = gelu_tanh(up_f).astype(BF)
    _, gelu_pull = jax.vjp(gelu_tanh, up_f)
    d_up = gelu_pull(d_act)[0].astype(BF)

    mixed, d_q, d_k, d_v = [], [], [], []
    for m in range(micro_count):
        allowed = (
            (seg[m][:, None] == seg[m][None, :])
            & (order[None, :] <= order[:, None])
            & ((valid[m][None, :] > 0) | (order[None, :] == order[:, None]))
        )
        scores = jnp.einsum("qhd,khd->hqk", queries[m], keys[m], preferred_element_type=F32) * scale
        masked = jnp.where(allowed[None], scores, -1e30)
        top = jnp.max(masked, axis=-1, keepdims=True)
        ex = jnp.exp(masked - top)
        probs = ex / jnp.sum(ex, axis=-1, keepdims=True)
        low = probs.astype(BF)
        mixed.append(
            jnp.einsum("hqk,khd->qhd", low, values[m], preferred_element_type=F32).reshape(
                row_len, 256
            )
        )
        d_probs = jnp.einsum("qhd,khd->hqk", d_heads[m], values[m], preferred_element_type=F32)
        total = jnp.sum(probs * d_probs, axis=-1, keepdims=True)
        d_scores = (probs * (d_probs - total)).astype(BF)
        d_q.append(
            jnp.einsum("hqk,khd->qhd", d_scores, keys[m], preferred_element_type=F32) * scale
        )
        d_k.append(
            jnp.einsum("hqk,qhd->khd", d_scores, queries[m], preferred_element_type=F32) * scale
        )
        d_v.append(jnp.einsum("hqk,qhd->khd", low, d_heads[m], preferred_element_type=F32))
    mixed = jnp.stack(mixed).astype(BF)
    _, rotate_pull = jax.vjp(rotate_local, raw_q)
    flat = (micro_count, row_len, 256)
    d_qkv = jnp.concatenate(
        [
            rotate_pull(jnp.stack(d_q))[0].reshape(flat),
            rotate_pull(jnp.stack(d_k))[0].reshape(flat),
            jnp.stack(d_v).reshape(flat),
        ],
        axis=-1,
    ).astype(BF)

    partial = jnp.dot(act, w_dn, preferred_element_type=F32) + jnp.dot(
        mixed, w_o, preferred_element_type=F32
    )
    partial = partial.astype(BF).reshape(micro_count, NZ, group, width)
    sums = reduce_ring([partial[0, k] for k in range(NZ)], [partial[1, k] for k in range(NZ)], send_z)
    out_hidden = (hidden_in.astype(F32) + (jnp.stack(sums) + b_sum)[:, None]).astype(BF)

    grad_mlp = jnp.concatenate(
        [
            jnp.einsum("mci,mcj->ij", normed, d_up, preferred_element_type=F32).astype(BF),
            jnp.einsum("mci,mcj->ij", act, cot, preferred_element_type=F32).astype(BF),
        ],
        axis=1,
    )
    grad_qkv = jnp.einsum("mci,mcj->ij", normed, d_qkv, preferred_element_type=F32).astype(BF)
    grad_out = jnp.einsum("mci,mcj->ij", mixed, cot, preferred_element_type=F32).astype(BF)
    grad_out = grad_out.reshape(32, 8, 4, 256).transpose(0, 2, 1, 3).reshape(1024, 256)

    d_normed = jnp.einsum("mcj,ij->mci", d_up, w_in[:, :1024], preferred_element_type=F32)
    d_normed = d_normed + jnp.einsum("mcj,ij->mci", d_qkv, w_in[:, 1024:], preferred_element_type=F32)
    sum_gain = jnp.sum(d_normed * xhat, axis=(0, 1))
    sum_shift = jnp.sum(d_normed, axis=(0, 1))
    sum_bqkv = jnp.sum(d_qkv.astype(F32), axis=(0, 1)).reshape(3, 4, 1, 64)
    sum_bup = jnp.sum(d_up.astype(F32), axis=(0, 1)).reshape(32, 1, 32)
    sum_cot = jnp.sum(cotangent.astype(F32), axis=(0, 1, 2)).reshape(32, 4, 8)
    mine = jnp.arange(4) == z
    sum_bqkv = jnp.where(mine[None, None, :, None], sum_bqkv, 0.0).reshape(32, 4, 24)
    sum_bup = jnp.where(mine[None, :, None], sum_bup, 0.0)
    vec_grads = jnp.concatenate(
        [
            sum_bqkv,
            sum_cot,
            sum_bup,
            sum_cot,
            sum_gain.reshape(32, 4, 8),
            sum_shift.reshape(32, 4, 8),
        ],
        axis=-1,
    ).astype(BF)
    vec_grads = jnp.pad(vec_grads[:, :, None, :], ((0, 0), (0, 0), (0, 7), (0, 40)))
    grad_att = jnp.concatenate([grad_qkv, grad_out, vec_grads.reshape(1024, 128)], axis=1)

    d_part = d_normed.astype(BF).reshape(micro_count, NZ, group, width)
    d_sums = reduce_ring([d_part[0, k] for k in range(NZ)], [d_part[1, k] for k in range(NZ)], send_z)
    own_xhat = xhat[:, :group]
    own_r = rs[:, :group]
    grads_n = jnp.stack(d_sums) * gain
    mean_g = jnp.mean(grads_n, axis=-1, keepdims=True)
    mean_gx = jnp.mean(grads_n * own_xhat, axis=-1, keepdims=True)
    grad_input = cotangent.astype(F32) + (own_r * (grads_n - mean_g - own_xhat * mean_gx))[:, None]

    red_mlp = reduce_dp(grad_mlp, place)
    red_att = reduce_dp(grad_att, place)
    final_down = red_mlp[:, 1024:]
    back = jnp.concatenate([red_mlp[:, :1024], red_att[:, :768], red_att[:, 1024:]], axis=1)
    back = lax.all_to_all(back.reshape(4, 8, 1920), "seq", 0, 0, tiled=True)
    final_up = back[..., :1024].reshape(4, 8, 32, 32).transpose(1, 2, 0, 3).reshape(8, 4096)
    final_qkv = back[..., 1024:1792].reshape(4, 8, 3, 4, 64).transpose(1, 2, 3, 0, 4)
    final_qkv = final_qkv.reshape(8, 3072)
    final_vec = jnp.sum(back[:, 0, 1792:1880], axis=0)
    final_out = red_att[:, 768:1024].reshape(4, 8, 256).transpose(1, 0, 2).reshape(8, 1024)
    final_out = lax.ppermute(final_out, ("dp", "seq"), from_heads)
    return (
        out_hidden,
        grad_input,
        final_qkv,
        final_out,
        final_up,
        final_down,
        final_vec[:24],
        final_vec[24:32],
        final_vec[32:64],
        final_vec[64:72],
        final_vec[72:80],
        final_vec[80:88],
    )


def solution(mesh):
    rows = P(None, "dp", "seq", None)
    tokens = P(None, "dp", None)
    matrix = P(("dp", "seq"), None)
    vector = P(("dp", "seq"))
    in_specs = (rows, tokens, tokens) + (matrix,) * 4 + (vector,) * 6 + (rows,)
    out_specs = (rows, rows) + (matrix,) * 4 + (vector,) * 6
    return jax.shard_map(body, mesh=mesh, in_specs=in_specs, out_specs=out_specs, check_vma=False)
```

time: 2770 us -> 566 us (0.20)
  waiting for transfers between devices: 2300 us -> 127 us
  blocking collectives: 136 us -> 0 us
  starting transfers between devices: 0.48 us -> 120 us
    reduce_scatter x6 -> x0, waiting for transfers between devices: 2180 us -> none  [the longest x1 665 us: body(): lax.psum_scatter(grad_up, ('dp', 'seq'), scatter_dimension=0, tiled=True)]
    unnamed x2 -> x0, blocking collectives: 136 us -> none
    all_gather x6 -> x1, waiting for transfers between devices: 117 us -> 0.01 us  [body(): weights = lax.all_gather(payload, 'dp', axis=0, tiled=True)]
    ppermute x0 -> x76, waiting for transfers between devices: none -> 117 us  [the longest x24 82.3 us: send_z(): return lax.ppermute(value, 'seq', [(i, (i + step) % NZ) for i in range(NZ)])]
    ppermute x0 -> x76, starting transfers between devices: none -> 111 us  [the longest x50 66.4 us: send_dp(): return lax.ppermute(value, 'dp', pairs)]
    dot_general x24 -> x21, matrix products: 180 us -> 136 us  [the longest x2 18.9 us: body(): jnp.einsum('hqk,qhd->khd', low, d_heads[m], preferred_element_type=F32)]
  transfers between devices with their start and end apart: 12 -> 79, of which waited for: 9 -> 30; matrix products, arithmetic and copies ran while one was open for 11% -> 9% of each run, Pallas kernels for 0% -> 0%
where the time goes in v1:
time: 566 us; the launch traced here: 558 us
  matrix products  158 us (28%)
  waiting for transfers between devices  127 us (22%)
  starting transfers between devices  120 us (21%)
  other arithmetic  70.2 us (12%)
  local copies, waits for them, and re-layouts  65.9 us (12%)
  between operations  16.5 us (3%)
    ppermute x24, waiting for transfers between devices, send_z(): return lax.ppermute(value, 'seq', [(i, (i + step) % NZ) for i in range(NZ)])  82.3 us
    ppermute x50, starting transfers between devices, send_dp(): return lax.ppermute(value, 'dp', pairs)  66.4 us
    ppermute x24, starting transfers between devices, send_z(): return lax.ppermute(value, 'seq', [(i, (i + step) % NZ) for i in range(NZ)])  42.9 us
    ppermute x50, waiting for transfers between devices, send_dp(): return lax.ppermute(value, 'dp', pairs)  34.3 us
    sub x2, matrix products, body(): ex = jnp.exp(masked - top)  22.6 us
    convert_element_type x2, other arithmetic, body(): d_scores = (probs * (d_probs - total)).astype(BF)  19.6 us
    dot_general x2, matrix products, body(): jnp.einsum('hqk,qhd->khd', low, d_heads[m], preferred_element_type=F32)  18.9 us
    dot_general x2, matrix products, body(): jnp.einsum('qhd,khd->hqk', d_heads[m], values[m], preferred_element_type=...  17.7 us
  transfers between devices with their start and end apart: 79, of which 30 were waited for; matrix products, arithmetic and copies ran while one was open for 9% of the time, Pallas kernels for 0%

profile of v1, /device:TPU:0, one launch (start us, length us, event | category | flops | bytes accessed | tf_op | source)
XLA Modules:
  0.0 557.9 jit_solution(14476727431380899341)
XLA Ops:
  9.8 4.1 concatenate.128
  14.6 5.4 all-to-all-start
  21.3 4.6 all-to-all-done
  28.8 2.9 collective-permute-start.1
  31.7 3.7 collective-permute-start
  40.3 3.8 fusion.29
  44.6 3.5 collective-permute-done.1
  51.1 8.3 %collective-permute-done.5 = bf16[256,1024]{1,0:T(8,128)(2,1)} collective-permute-done((bf16[256,1024]{1,0:T(8,128)(2,1)S(1)}, bf16[256,1024]{1,0:T(8,128)(2,1)}, u32[]{:S(2)}, u32[]{:S(2)}) %collective-permute-start.5) | collective-permute-done | bytes 524320 | tf_op jit(solution)/shard_map/ppermute | solution.py:46
  62.9 7.8 %collective-permute-done.14 = bf16[256,1024]{1,0:T(8,128)(2,1)} collective-permute-done((bf16[256,1024]{1,0:T(8,128)(2,1)}, bf16[256,1024]{1,0:T(8,128)(2,1)}, u32[]{:S(2)}, u32[]{:S(2)}) %collective-permute-start.14) | collective-permute-done | bytes 524320 | tf_op jit(solution)/shard_map/ppermute | solution.py:46
  75.7 6.2 %collective-permute-done.2 = bf16[256,1024]{1,0:T(8,128)(2,1)} collective-permute-done((bf16[256,1024]{1,0:T(8,128)(2,1)S(1)}, bf16[256,1024]{1,0:T(8,128)(2,1)}, u32[]{:S(2)}, u32[]{:S(2)}) %collective-permute-start.2) | collective-permute-done | bytes 524320 | tf_op jit(solution)/shard_map/ppermute | solution.py:46
  85.7 8.3 %collective-permute-done.4 = bf16[256,1024]{1,0:T(8,128)(2,1)} collective-permute-done((bf16[256,1024]{1,0:T(8,128)(2,1)}, bf16[256,1024]{1,0:T(8,128)(2,1)}, u32[]{:S(2)}, u32[]{:S(2)}) %collective-permute-start.4) | collective-permute-done | bytes 524320 | tf_op jit(solution)/shard_map/ppermute | solution.py:46
  95.6 3.8 maximum_bitcast_fusion.2
  99.4 3.2 collective-permute-done.18
  102.5 2.6 maximum_bitcast_fusion.3
  112.1 3.7 convolution_convert_fusion
  117.0 10.6 %fusion.31 = f32[2,1024,1792]{2,1,0:T(8,128)S(1)} fusion(bf16[1024,3200]{1,0:T(8,128)(2,1)} %all-gather.2.cloned.1.call-done, f32[1024]{0:T(1024)S(1)} %add.501, f32[1024]{0:T(1024)S(1)} %mul.273, f32[2,1024]{1,0:T(2,128)S(1)} %get-tuple-element.155, f32[2,1024]{1,0:T(2,128)S(1)} %broadcast_multiply_fusion, bf16[1,1024,1024]{2,1,0:T(8,128)(2,1)S(1)} %copy-done.3, ...), kind=kOutput, calls=%fused_computation.64 | convolution fusion | flops 7530872832 | bytes 22568960 | tf_op jit(solution)/shard_map/dot_general | solution.py:195
  127.5 3.7 fusion.161
  131.3 3.2 copy-done.29
  135.6 4.0 fusion.162
  139.6 2.9 copy.73
  149.2 11.4 %fusion.170 = (f32[4,1024]{1,0:T(4,128)S(1)}, f32[4,1024,1024]{1,2,0:T(8,128)}) fusion(pred[1024,1024]{0,1:T(8,128)(4,1)} %get-tuple-element.158, bf16[2,1024,4,64]{1,3,2,0:T(8,128)(2,1)S(1)} %get-tuple-element.177, bf16[2,1024,4,64]{1,3,2,0:T(8,128)(2,1)S(1)} %get-tuple-element.178), kind=kOutput, calls=%fused_computation.452 | convolution fusion | flops 553649152 | bytes 18890752 | tf_op jit(solution)/shard_map/sub | solution.py:239
  160.6 9.4 %fusion.49 = bf16[4,64,1024]{2,1,0:T(8,128)(2,1)} fusion(bf16[1024,4,64]{0,2,1:T(8,128)(2,1)S(1)} %bitcast.602, f32[4,1024,1024]{1,2,0:T(8,128)} %get-tuple-element.167, f32[4,1024]{1,0:T(4,128)S(1)} %get-tuple-element.166), kind=kOutput, calls=%fused_computation.111 | convolution fusion | flops 545521664 | bytes 17842176 | tf_op jit(solution)/shard_map/hqk,qhd->khd/dot_general | solution.py:256
  171.3 2.5 fusion.46
  173.8 7.2 %multiply_reduce_fusion.1 = (f32[4,1024]{1,0:T(4,128)S(1)}, f32[4,1024,1024]{1,2,0:T(8,128)}) fusion(f32[4,1024,1024]{1,2,0:T(8,128)S(1)} %copy-done.11, f32[4,1024]{1,0:T(4,128)S(1)} %get-tuple-element.166, bf16[1024,4,64]{0,2,1:T(8,128)(2,1)S(1)} %bitcast.603, bf16[1024,4,64]{0,2,1:T(8,128)(2,1)S(1)} %bitcast.596), kind=kOutput, calls=%fused_computation.5 | convolution fusion | flops 549449728 | bytes 34635776 | tf_op jit(solution)/shard_map/qhd,khd->hqk/dot_general | solution.py:247
  181.0 7.9 %multiply_convert_fusion.1 = bf16[4,1024,1024]{1,2,0:T(8,128)(2,1)S(1)} fusion(f32[4,1024,1024]{1,2,0:T(8,128)} %get-tuple-element.171, f32[4,1024]{1,0:T(4,128)S(1)} %get-tuple-element.170, f32[4,1024,1024]{1,2,0:T(8,128)S(1)} %copy-done.11, f32[4,1024]{1,0:T(4,128)S(1)} %get-tuple-element.166), kind=kLoop, calls=%fused_computation.4 | loop fusion | flops 16777216 | bytes 41975808 | tf_op jit(solution)/shard_map/convert_element_type | solution.py:249
  189.0 2.7 fusion.43
  195.3 11.3 %fusion.169 = (f32[4,1024]{1,0:T(4,128)S(1)}, f32[4,1024,1024]{1,2,0:T(8,128)}) fusion(pred[1024,1024]{0,1:T(8,128)(4,1)} %get-tuple-element.159, bf16[2,1024,4,64]{1,3,2,0:T(8,128)(2,1)} %copy-done.19, bf16[2,1024,4,64]{1,3,2,0:T(8,128)(2,1)S(1)} %get-tuple-element.178), kind=kOutput, calls=%fused_computation.451 | convolution fusion | flops 553649152 | bytes 18890752 | tf_op jit(solution)/shard_map/sub | solution.py:239
  206.6 9.5 %fusion.55 = bf16[4,64,1024]{2,1,0:T(8,128)(2,1)} fusion(bf16[1024,4,64]{0,2,1:T(8,128)(2,1)} %bitcast.600, f32[4,1024,1024]{1,2,0:T(8,128)} %get-tuple-element.165, f32[4,1024]{1,0:T(4,128)S(1)} %get-tuple-element.164), kind=kOutput, calls=%fused_computation.113 | convolution fusion | flops 545521664 | bytes 17842176 | tf_op jit(solution)/shard_map/hqk,qhd->khd/dot_general | solution.py:256
  219.9 10.5 %multiply_reduce_fusion = (f32[4,1024]{1,0:T(4,128)S(1)}, f32[4,1024,1024]{1,2,0:T(8,128)}) fusion(f32[4,1024,1024]{1,2,0:T(8,128)} %get-tuple-element.165, f32[4,1024]{1,0:T(4,128)S(1)} %get-tuple-element.164, bf16[1024,4,64]{0,2,1:T(8,128)(2,1)S(1)} %bitcast.601, bf16[1024,4,64]{0,2,1:T(8,128)(2,1)S(1)} %bitcast.599), kind=kOutput, calls=%fused_computation.3 | convolution fusion | flops 549449728 | bytes 34635776 | tf_op jit(solution)/shard_map/qhd,khd->hqk/dot_general | solution.py:247
  230.4 11.7 %multiply_convert_fusion = bf16[4,1024,1024]{1,2,0:T(8,128)(2,1)S(1)} fusion(f32[4,1024,1024]{1,2,0:T(8,128)} %get-tuple-element.169, f32[4,1024]{1,0:T(4,128)S(1)} %get-tuple-element.168, f32[4,1024,1024]{1,2,0:T(8,128)} %get-tuple-element.165, f32[4,1024]{1,0:T(4,128)S(1)} %get-tuple-element.164), kind=kLoop, calls=%fused_computation.2 | loop fusion | flops 16777216 | bytes 41975808 | tf_op jit(solution)/shard_map/convert_element_type | solution.py:249
  242.2 2.7 fusion.42
  262.4 7.8 %bitcast_convert_fusion.2 = bf16[1024,768]{1,0:T(8,128)(2,1)} fusion(f32[1024]{0:T(1024)S(1)} %copy-done.63, f32[1024]{0:T(1024)S(1)} %copy-done.53, f32[2,1024]{1,0:T(2,128)S(1)} %copy-done.60, f32[2,1024]{1,0:T(2,128)S(1)} %copy-done.55, bf16[1,1024,256]{2,1,0:T(8,128)(2,1)} %copy.87, bf16[1,1024,256]{2,1,0:T(8,128)(2,1)} %copy.86, ...), kind=kOutput, calls=%fused_computation.66 | convolution fusion | flops 3249274880 | bytes 8937472 | tf_op jit(solution)/shard_map/mci,mcj->ij/dot_general | solution.py:283
  271.8 11.3 %bitcast_convert_fusion = bf16[1024,1024]{0,1:T(8,128)(2,1)} fusion(bf16[1,1024,1024]{2,1,0:T(8,128)(2,1)} %maximum_bitcast_fusion.3, bf16[1,1024,1024]{2,1,0:T(8,128)(2,1)} %maximum_bitcast_fusion.2, f32[2,1024,1792]{2,1,0:T(8,128)} %copy-done.29, f32[1024]{0:T(1024)S(1)} %add.505), kind=kOutput, calls=%fused_computation.51 | convolution fusion | flops 4319084544 | bytes 14684160 | tf_op jit(solution)/shard_map/mci,mcj->ij/dot_general | solution.py:279
  283.2 13.4 %convert_reduce_fusion.1 = (bf16[1024]{0:T(1024)(128)(2,1)S(1)}, bf16[2,1024,1024]{2,1,0:T(8,128)(2,1)}) fusion(f32[1024]{0:T(1024)S(1)} %add.505, f32[2,1024,1792]{2,1,0:T(8,128)} %copy-done.29, bf16[1024,3200]{1,0:T(8,128)(2,1)} %all-gather.2.cloned.1.call-done, bf16[1,1024,1024]{2,1,0:T(8,128)(2,1)S(1)} %copy-done.35, ...), kind=kOutput, calls=%fused_computation.28 | convolution fusion | flops 4345297920 | bytes 18880512 | tf_op jit(solution)/shard_map/mcj,ij->mci/dot_general | solution.py:224
  296.7 8.3 %bitcast_convert_fusion.1 = bf16[1024,1024]{0,1:T(8,128)(2,1)S(1)} fusion(bf16[2,1024,1024]{2,1,0:T(8,128)(2,1)} %get-tuple-element.173, f32[1024]{0:T(1024)S(1)} %copy-done.63, f32[1024]{0:T(1024)S(1)} %copy-done.53, f32[2,1024]{1,0:T(2,128)S(1)} %copy-done.60, f32[2,1024]{1,0:T(2,128)S(1)} %copy-done.55, bf16[1,1024,1024]{2,1,0:T(8,128)(2,1)} %copy-done.2, ...), kind=kOutput, calls=%fused_computation.52 | convolution fusion | flops 4310695936 | bytes 10510336 | tf_op jit(solution)/shard_map/mci,mcj->ij/dot_general | solution.py:278
  307.4 6.5 %copy.92 = bf16[1024,2048]{1,0:T(8,128)(2,1)} copy(bf16[1024,2048]{0,1:T(8,128)(2,1)} %pad_maximum_fusion.2) | data formatting | bytes 8388608 | tf_op jit(solution)/shard_map/concatenate | solution.py:276
  318.0 4.7 fusion.58
  322.7 8.9 %fusion.41 = f32[2,1024,1024]{2,1,0:T(8,128)S(1)} fusion(bf16[1024,3200]{1,0:T(8,128)(2,1)} %all-gather.2.cloned.1.call-done, f32[2,1024,1792]{2,1,0:T(8,128)} %copy-done.29, f32[1024]{0:T(1024)S(1)} %add.505), kind=kOutput, calls=%fused_computation.98 | convolution fusion | flops 4315938816 | bytes 18878464 | tf_op jit(solution)/shard_map/dot_general | solution.py:269
  341.7 7.2 %fusion.33 = f32[2,1024,1024]{2,1,0:T(8,128)S(1)} fusion(bf16[2,1024,1024]{2,1,0:T(8,128)(2,1)} %get-tuple-element.173, bf16[1024,3200]{1,0:T(8,128)(2,1)} %all-gather.2.cloned.1.call-done), kind=kOutput, calls=%fused_computation.80 | convolution fusion | flops 4294967296 | bytes 14680064 | tf_op jit(solution)/shard_map/mcj,ij->mci/dot_general | solution.py:287
  348.9 8.5 %fusion.160 = (bf16[1024]{0:T(1024)(128)(2,1)S(1)}, bf16[1024]{0:T(1024)(128)(2,1)S(1)}, bf16[2,1024,1024]{2,1,0:T(8,128)(2,1)}, f32[2,1024,1024]{2,1,0:T(8,128)}) fusion(f32[2,1024]{1,0:T(2,128)S(1)} %copy-done.60, f32[2,1024]{1,0:T(2,128)S(1)} %copy-done.55, bf16[1,1024,1024]{2,1,0:T(8,128)(2,1)S(1)} %copy-done.4, ...), kind=kOutput, calls=%fused_computation.442 | convolution fusion | flops 3256875008 | bytes 29904896 | tf_op jit(solution)/shard_map/mcj,ij->mci/dot_general | solution.py:288
  360.6 3.1 collective-permute-start.23
  365.0 7.2 %collective-permute-done.19 = bf16[256,1024]{1,0:T(8,128)(2,1)S(1)} collective-permute-done((bf16[256,1024]{1,0:T(8,128)(2,1)S(1)}, bf16[256,1024]{1,0:T(8,128)(2,1)S(1)}, u32[]{:S(2)}, u32[]{:S(2)}) %collective-permute-start.19) | collective-permute-done | bytes 524320 | tf_op jit(solution)/shard_map/ppermute | solution.py:46
  372.4 3.3 collective-permute-start.21
  376.0 12.3 %collective-permute-done.8 = bf16[256,1024]{1,0:T(8,128)(2,1)S(1)} collective-permute-done((bf16[256,1024]{1,0:T(8,128)(2,1)S(1)}, bf16[256,1024]{1,0:T(8,128)(2,1)S(1)}, u32[]{:S(2)}, u32[]{:S(2)}) %collective-permute-start.8) | collective-permute-done | bytes 524320 | tf_op jit(solution)/shard_map/ppermute | solution.py:46
  390.1 9.4 %collective-permute-done.20 = bf16[256,1024]{1,0:T(8,128)(2,1)S(1)} collective-permute-done((bf16[256,1024]{1,0:T(8,128)(2,1)S(1)}, bf16[256,1024]{1,0:T(8,128)(2,1)S(1)}, u32[]{:S(2)}, u32[]{:S(2)}) %collective-permute-start.20) | collective-permute-done | bytes 524320 | tf_op jit(solution)/shard_map/ppermute | solution.py:46
  400.8 2.5 collective-permute-start.53
  403.5 3.2 collective-permute-start.55
  408.8 3.1 collective-permute-start.43
  411.9 2.5 collective-permute-done.43
  414.4 3.6 collective-permute-start.56
  420.3 3.5 collective-permute-start.44
  427.8 4.1 collective-permute-done.52
  434.3 3.2 collective-permute-start.61
  439.3 3.3 collective-permute-start.49
  444.3 3.3 collective-permute-start.62
  457.4 7.9 %collective-permute-start.12 = (bf16[256,1024]{1,0:T(8,128)(2,1)S(1)}, bf16[256,1024]{1,0:T(8,128)(2,1)S(1)}, u32[]{:S(2)}, u32[]{:S(2)}) collective-permute-start(bf16[256,1024]{1,0:T(8,128)(2,1)S(1)} %get-tuple-element.71), channel_id=1, source_target_pairs={{0,3},{1,0},{2,1},{3,2},{4,7},{5,4},{6,5},{7,6},{8,11},{9,8},{10,9... | collective-permute-start | bytes 1572872 | tf_op jit(solution)/shard_map/ppermute | solution.py:46
  466.1 3.9 collective-permute-done.10
  470.0 12.1 %collective-permute-done.12 = bf16[256,1024]{1,0:T(8,128)(2,1)S(1)} collective-permute-done((bf16[256,1024]{1,0:T(8,128)(2,1)S(1)}, bf16[256,1024]{1,0:T(8,128)(2,1)S(1)}, u32[]{:S(2)}, u32[]{:S(2)}) %collective-permute-start.12) | collective-permute-done | bytes 524320 | tf_op jit(solution)/shard_map/ppermute | solution.py:46
  494.4 3.7 collective-permute-done.30
  506.1 3.3 collective-permute-done.26
  519.5 4.9 collective-permute-done.32
  528.6 3.3 collective-permute-start.37
  536.1 3.4 all-to-all-start.1
  540.3 5.8 %all-to-all-done.1 = f32[4,8,1920]{2,1,0:T(8,128)S(1)} async-done(((f32[4,8,1920]{2,1,0:T(8,128)}), f32[4,8,1920]{2,1,0:T(8,128)S(1)}, u32[]{:S(2)}, u32[]{:S(2)}) %all-to-all-start.1) | async-done | bytes 245792 | tf_op jit(solution)/shard_map/all_to_all | solution.py:324
  (441 shorter events, 166.0 us)
Async XLA Ops:
  14.6 11.3 %all-to-all-start = ((bf16[4,8,1920]{2,1,0:T(8,128)(2,1)}), bf16[4,8,1920]{2,1,0:T(8,128)(2,1)S(1)}, u32[]{:S(2)}, u32[]{:S(2)}) async-start(bf16[4,8,1920]{2,1,0:T(8,128)(2,1)} %pad_maximum_fusion.14), calls=%async_computation | async-start | bytes 245760 | tf_op jit(solution)/shard_map/all_to_all | solution.py:156
  20.0 88.0 %all-gather.2.cloned.1.call-start = ((), (), s32[]{:S(2)}) async-start(), calls=%async_computation.2 | async-start | bytes 6758400 | tf_op jit(solution)/shard_map/all_gather | solution.py:169
  20.0 5.9 %collective-permute-start.6 = (bf16[8,1024]{1,0:T(8,128)(2,1)}, bf16[8,1024]{1,0:T(8,128)(2,1)S(1)}, u32[]{:S(2)}, u32[]{:S(2)}) collective-permute-start(bf16[8,1024]{1,0:T(8,128)(2,1)} %param.20), channel_id=1, source_target_pairs={{0,0},{1,4},{2,8},{3,12},{4,16},{5,20},{6,24},{7,28},{8,1},{9,5},{... | collective-permute-start | bytes 49160 | tf_op jit(solution)/shard_map/ppermute | solution.py:166
  28.8 19.3 %collective-permute-start.1 = (bf16[256,1024]{1,0:T(8,128)(2,1)S(1)}, bf16[256,1024]{1,0:T(8,128)(2,1)S(1)}, u32[]{:S(2)}, u32[]{:S(2)}) collective-permute-start(bf16[256,1024]{1,0:T(8,128)(2,1)S(1)} %get-tuple-element.101), channel_id=1, source_target_pairs={{0,1},{1,2},{2,3},{3,0},{4,5},{5,6},{6,7},{7,4},{8,9},{9,10},{10,1... | collective-permute-start | bytes 1572872 | tf_op jit(solution)/shard_map/ppermute | solution.py:46
  31.7 18.5 %collective-permute-start = (bf16[256,1024]{1,0:T(8,128)(2,1)S(1)}, bf16[256,1024]{1,0:T(8,128)(2,1)}, u32[]{:S(2)}, u32[]{:S(2)}) collective-permute-start(bf16[256,1024]{1,0:T(8,128)(2,1)S(1)} %get-tuple-element.101), channel_id=1, source_target_pairs={{0,3},{1,0},{2,1},{3,2},{4,7},{5,4},{6,5},{7,6},{8,11},{9,8},{10,9... | collective-permute-start | bytes 1572872 | tf_op jit(solution)/shard_map/ppermute | solution.py:46
  35.4 24.1 %collective-permute-start.5 = (bf16[256,1024]{1,0:T(8,128)(2,1)S(1)}, bf16[256,1024]{1,0:T(8,128)(2,1)}, u32[]{:S(2)}, u32[]{:S(2)}) collective-permute-start(bf16[256,1024]{1,0:T(8,128)(2,1)S(1)} %get-tuple-element.102), channel_id=1, source_target_pairs={{0,1},{1,2},{2,3},{3,0},{4,5},{5,6},{6,7},{7,4},{8,9},{9,10},{10,1... | collective-permute-start | bytes 1572872 | tf_op jit(solution)/shard_map/ppermute | solution.py:46
  36.1 25.4 %collective-permute-start.3 = (bf16[256,1024]{1,0:T(8,128)(2,1)S(1)}, bf16[256,1024]{1,0:T(8,128)(2,1)}, u32[]{:S(2)}, u32[]{:S(2)}) collective-permute-start(bf16[256,1024]{1,0:T(8,128)(2,1)S(1)} %get-tuple-element.102), channel_id=1, source_target_pairs={{0,3},{1,0},{2,1},{3,2},{4,7},{5,4},{6,5},{7,6},{8,11},{9,8},{10,9... | collective-permute-start | bytes 1572872 | tf_op jit(solution)/shard_map/ppermute | solution.py:46
  39.5 31.2 %collective-permute-start.14 = (bf16[256,1024]{1,0:T(8,128)(2,1)}, bf16[256,1024]{1,0:T(8,128)(2,1)}, u32[]{:S(2)}, u32[]{:S(2)}) collective-permute-start(bf16[256,1024]{1,0:T(8,128)(2,1)} %get-tuple-element.99), channel_id=1, source_target_pairs={{0,1},{1,2},{2,3},{3,0},{4,5},{5,6},{6,7},{7,4},{8,9},{9,10},{10,1... | collective-permute-start | bytes 1572872 | tf_op jit(solution)/shard_map/ppermute | solution.py:46
  48.1 25.1 %collective-permute-start.16 = (bf16[256,1024]{1,0:T(8,128)(2,1)S(1)}, bf16[256,1024]{1,0:T(8,128)(2,1)}, u32[]{:S(2)}, u32[]{:S(2)}) collective-permute-start(bf16[256,1024]{1,0:T(8,128)(2,1)S(1)} %get-tuple-element.100), channel_id=1, source_target_pairs={{0,3},{1,0},{2,1},{3,2},{4,7},{5,4},{6,5},{7,6},{8,11},{9,8},{10,9... | collective-permute-start | bytes 1572872 | tf_op jit(solution)/shard_map/ppermute | solution.py:46
  50.2 31.8 %collective-permute-start.2 = (bf16[256,1024]{1,0:T(8,128)(2,1)S(1)}, bf16[256,1024]{1,0:T(8,128)(2,1)}, u32[]{:S(2)}, u32[]{:S(2)}) collective-permute-start(bf16[256,1024]{1,0:T(8,128)(2,1)S(1)} %collective-permute-done.1), channel_id=1, source_target_pairs={{0,1},{1,2},{2,3},{3,0},{4,5},{5,6},{6,7},{7,4},{8,9},{9,10},{10,1... | collective-permute-start | bytes 1572872 | tf_op jit(solution)/shard_map/ppermute | solution.py:46
  59.5 36.1 %collective-permute-start.13 = (bf16[256,1024]{1,0:T(8,128)(2,1)}, bf16[256,1024]{1,0:T(8,128)(2,1)}, u32[]{:S(2)}, u32[]{:S(2)}) collective-permute-start(bf16[256,1024]{1,0:T(8,128)(2,1)} %get-tuple-element.99), channel_id=1, source_target_pairs={{0,3},{1,0},{2,1},{3,2},{4,7},{5,4},{6,5},{7,6},{8,11},{9,8},{10,9... | collective-permute-start | bytes 1572872 | tf_op jit(solution)/shard_map/ppermute | solution.py:46
  61.5 32.5 %collective-permute-start.4 = (bf16[256,1024]{1,0:T(8,128)(2,1)}, bf16[256,1024]{1,0:T(8,128)(2,1)}, u32[]{:S(2)}, u32[]{:S(2)}) collective-permute-start(bf16[256,1024]{1,0:T(8,128)(2,1)} %collective-permute-done.3), channel_id=1, source_target_pairs={{0,3},{1,0},{2,1},{3,2},{4,7},{5,4},{6,5},{7,6},{8,11},{9,8},{10,9... | collective-permute-start | bytes 1572872 | tf_op jit(solution)/shard_map/ppermute | solution.py:46
  70.7 24.9 %collective-permute-start.15 = (bf16[256,1024]{1,0:T(8,128)(2,1)}, bf16[256,1024]{1,0:T(8,128)(2,1)}, u32[]{:S(2)}, u32[]{:S(2)}) collective-permute-start(bf16[256,1024]{1,0:T(8,128)(2,1)} %collective-permute-done.14), channel_id=1, source_target_pairs={{0,1},{1,2},{2,3},{3,0},{4,5},{5,6},{6,7},{7,4},{8,9},{9,10},{10,1... | collective-permute-start | bytes 1572872 | tf_op jit(solution)/shard_map/ppermute | solution.py:46
  73.3 29.3 %collective-permute-start.18 = (bf16[256,1024]{1,0:T(8,128)(2,1)S(1)}, bf16[256,1024]{1,0:T(8,128)(2,1)S(1)}, u32[]{:S(2)}, u32[]{:S(2)}) collective-permute-start(bf16[256,1024]{1,0:T(8,128)(2,1)S(1)} %get-tuple-element.100), channel_id=1, source_target_pairs={{0,1},{1,2},{2,3},{3,0},{4,5},{5,6},{6,7},{7,4},{8,9},{9,10},{10,1... | collective-permute-start | bytes 1572872 | tf_op jit(solution)/shard_map/ppermute | solution.py:46
  81.9 20.6 %collective-permute-start.17 = (bf16[256,1024]{1,0:T(8,128)(2,1)}, bf16[256,1024]{1,0:T(8,128)(2,1)S(1)}, u32[]{:S(2)}, u32[]{:S(2)}) collective-permute-start(bf16[256,1024]{1,0:T(8,128)(2,1)} %collective-permute-done.16), channel_id=1, source_target_pairs={{0,3},{1,0},{2,1},{3,2},{4,7},{5,4},{6,5},{7,6},{8,11},{9,8},{10,9... | collective-permute-start | bytes 1572872 | tf_op jit(solution)/shard_map/ppermute | solution.py:46
  336.2 24.4 %collective-permute-start.7 = (bf16[256,1024]{1,0:T(8,128)(2,1)}, bf16[256,1024]{1,0:T(8,128)(2,1)}, u32[]{:S(2)}, u32[]{:S(2)}) collective-permute-start(bf16[256,1024]{1,0:T(8,128)(2,1)} %get-tuple-element.72), channel_id=1, source_target_pairs={{0,1},{1,2},{2,3},{3,0},{4,5},{5,6},{6,7},{7,4},{8,9},{9,10},{10,1... | collective-permute-start | bytes 1572872 | tf_op jit(solution)/shard_map/ppermute | solution.py:46
  337.4 35.0 %collective-permute-start.11 = (bf16[256,1024]{1,0:T(8,128)(2,1)}, bf16[256,1024]{1,0:T(8,128)(2,1)}, u32[]{:S(2)}, u32[]{:S(2)}) collective-permute-start(bf16[256,1024]{1,0:T(8,128)(2,1)} %get-tuple-element.73), channel_id=1, source_target_pairs={{0,3},{1,0},{2,1},{3,2},{4,7},{5,4},{6,5},{7,6},{8,11},{9,8},{10,9... | collective-permute-start | bytes 1572872 | tf_op jit(solution)/shard_map/ppermute | solution.py:46
  339.5 36.3 %collective-permute-start.9 = (bf16[256,1024]{1,0:T(8,128)(2,1)}, bf16[256,1024]{1,0:T(8,128)(2,1)}, u32[]{:S(2)}, u32[]{:S(2)}) collective-permute-start(bf16[256,1024]{1,0:T(8,128)(2,1)} %get-tuple-element.75), channel_id=1, source_target_pairs={{0,3},{1,0},{2,1},{3,2},{4,7},{5,4},{6,5},{7,6},{8,11},{9,8},{10,9... | collective-permute-start | bytes 1572872 | tf_op jit(solution)/shard_map/ppermute | solution.py:46
  359.9 12.3 %collective-permute-start.19 = (bf16[256,1024]{1,0:T(8,128)(2,1)S(1)}, bf16[256,1024]{1,0:T(8,128)(2,1)S(1)}, u32[]{:S(2)}, u32[]{:S(2)}) collective-permute-start(bf16[256,1024]{1,0:T(8,128)(2,1)S(1)} %get-tuple-element.66), channel_id=1, source_target_pairs={{0,1},{1,2},{2,3},{3,0},{4,5},{5,6},{6,7},{7,4},{8,9},{9,10},{10,1... | collective-permute-start | bytes 1572872 | tf_op jit(solution)/shard_map/ppermute | solution.py:46
  360.5 39.5 %collective-permute-start.38 = (bf16[16,32,1152]{2,1,0:T(8,128)(2,1)S(1)}, bf16[16,32,1152]{2,1,0:T(8,128)(2,1)S(1)}, u32[]{:S(2)}, u32[]{:S(2)}) collective-permute-start(bf16[16,32,1152]{2,1,0:T(8,128)(2,1)S(1)} %dynamic-slice_bitcast_fusion.1), channel_id=1, source_target_pairs={{0,4},{4,0},{8,12},{12,8},{16,20},{20,16},{24,28},{28,24},{32,36},... | collective-permute-start | bytes 3538952 | tf_op jit(solution)/shard_map/ppermute | solution.py:56
  360.6 29.5 %collective-permute-start.23 = (bf16[256,1024]{1,0:T(8,128)(2,1)S(1)}, bf16[256,1024]{1,0:T(8,128)(2,1)S(1)}, u32[]{:S(2)}, u32[]{:S(2)}) collective-permute-start(bf16[256,1024]{1,0:T(8,128)(2,1)S(1)} %get-tuple-element.67), channel_id=1, source_target_pairs={{0,3},{1,0},{2,1},{3,2},{4,7},{5,4},{6,5},{7,6},{8,11},{9,8},{10,9... | collective-permute-start | bytes 1572872 | tf_op jit(solution)/shard_map/ppermute | solution.py:46
  372.2 16.1 %collective-permute-start.8 = (bf16[256,1024]{1,0:T(8,128)(2,1)S(1)}, bf16[256,1024]{1,0:T(8,128)(2,1)S(1)}, u32[]{:S(2)}, u32[]{:S(2)}) collective-permute-start(bf16[256,1024]{1,0:T(8,128)(2,1)S(1)} %fusion.71), channel_id=1, source_target_pairs={{0,1},{1,2},{2,3},{3,0},{4,5},{5,6},{6,7},{7,4},{8,9},{9,10},{10,1... | collective-permute-start | bytes 1572872 | tf_op jit(solution)/shard_map/ppermute | solution.py:46
  372.4 17.7 %collective-permute-start.21 = (bf16[256,1024]{1,0:T(8,128)(2,1)S(1)}, bf16[256,1024]{1,0:T(8,128)(2,1)S(1)}, u32[]{:S(2)}, u32[]{:S(2)}) collective-permute-start(bf16[256,1024]{1,0:T(8,128)(2,1)S(1)} %get-tuple-element.69), channel_id=1, source_target_pairs={{0,3},{1,0},{2,1},{3,2},{4,7},{5,4},{6,5},{7,6},{8,11},{9,8},{10,9... | collective-permute-start | bytes 1572872 | tf_op jit(solution)/shard_map/ppermute | solution.py:46
  375.7 23.8 %collective-permute-start.20 = (bf16[256,1024]{1,0:T(8,128)(2,1)S(1)}, bf16[256,1024]{1,0:T(8,128)(2,1)S(1)}, u32[]{:S(2)}, u32[]{:S(2)}) collective-permute-start(bf16[256,1024]{1,0:T(8,128)(2,1)S(1)} %fusion.65), channel_id=1, source_target_pairs={{0,1},{1,2},{2,3},{3,0},{4,5},{5,6},{6,7},{7,4},{8,9},{9,10},{10,1... | collective-permute-start | bytes 1572872 | tf_op jit(solution)/shard_map/ppermute | solution.py:46
  388.3 77.1 %collective-permute-start.22 = (bf16[256,1024]{1,0:T(8,128)(2,1)S(1)}, bf16[256,1024]{1,0:T(8,128)(2,1)S(1)}, u32[]{:S(2)}, u32[]{:S(2)}) collective-permute-start(bf16[256,1024]{1,0:T(8,128)(2,1)S(1)} %get-tuple-element.68), channel_id=1, source_target_pairs={{0,1},{1,2},{2,3},{3,0},{4,5},{5,6},{6,7},{7,4},{8,9},{9,10},{10,1... | collective-permute-start | bytes 1572872 | tf_op jit(solution)/shard_map/ppermute | solution.py:46
  400.8 27.0 %collective-permute-start.53 = (bf16[2,32,576]{2,1,0:T(8,128)(2,1)S(1)}, bf16[2,32,576]{2,1,0:T(8,128)(2,1)S(1)}, u32[]{:S(2)}, u32[]{:S(2)}) collective-permute-start(bf16[2,32,576]{2,1,0:T(8,128)(2,1)S(1)} %slice_bitcast_fusion.58), channel_id=1, source_target_pairs={{0,24},{4,28},{8,0},{12,4},{16,8},{20,12},{24,16},{28,20},{32,56},... | collective-permute-start | bytes 221192 | tf_op jit(solution)/shard_map/ppermute | solution.py:56
  403.3 14.7 %collective-permute-start.54 = (bf16[2,32,576]{2,1,0:T(8,128)(2,1)S(1)}, bf16[2,32,576]{2,1,0:T(8,128)(2,1)S(1)}, u32[]{:S(2)}, u32[]{:S(2)}) collective-permute-start(bf16[2,32,576]{2,1,0:T(8,128)(2,1)S(1)} %get-tuple-element.111), channel_id=1, source_target_pairs={{0,8},{4,12},{8,16},{12,20},{16,24},{20,28},{24,0},{28,4},{32,40},... | collective-permute-start | bytes 221192 | tf_op jit(solution)/shard_map/ppermute | solution.py:56
  403.4 15.0 %collective-permute-start.51 = (bf16[2,32,576]{2,1,0:T(8,128)(2,1)S(1)}, bf16[2,32,576]{2,1,0:T(8,128)(2,1)S(1)}, u32[]{:S(2)}, u32[]{:S(2)}) collective-permute-start(bf16[2,32,576]{2,1,0:T(8,128)(2,1)S(1)} %get-tuple-element.112), channel_id=1, source_target_pairs={{0,8},{4,12},{8,16},{12,20},{16,24},{20,28},{24,0},{28,4},{32,40},... | collective-permute-start | bytes 221192 | tf_op jit(solution)/shard_map/ppermute | solution.py:56
  408.8 5.6 %collective-permute-start.43 = (bf16[2,32,576]{2,1,0:T(8,128)(2,1)S(1)}, bf16[2,32,576]{2,1,0:T(8,128)(2,1)S(1)}, u32[]{:S(2)}, u32[]{:S(2)}) collective-permute-start(bf16[2,32,576]{2,1,0:T(8,128)(2,1)S(1)} %get-tuple-element.108), channel_id=1, source_target_pairs={{0,96},{4,100},{8,104},{12,108},{16,112},{20,116},{24,120},{28,124... | collective-permute-start | bytes 221192 | tf_op jit(solution)/shard_map/ppermute | solution.py:56
  414.4 5.9 %collective-permute-start.56 = (bf16[2,32,576]{2,1,0:T(8,128)(2,1)S(1)}, bf16[2,32,576]{2,1,0:T(8,128)(2,1)S(1)}, u32[]{:S(2)}, u32[]{:S(2)}) collective-permute-start(bf16[2,32,576]{2,1,0:T(8,128)(2,1)S(1)} %fusion.95), channel_id=1, source_target_pairs={{0,24},{4,28},{8,0},{12,4},{16,8},{20,12},{24,16},{28,20},{32,56},... | collective-permute-start | bytes 221192 | tf_op jit(solution)/shard_map/ppermute | solution.py:56
  418.1 6.2 %collective-permute-start.42 = (bf16[2,32,576]{2,1,0:T(8,128)(2,1)S(1)}, bf16[2,32,576]{2,1,0:T(8,128)(2,1)S(1)}, u32[]{:S(2)}, u32[]{:S(2)}) collective-permute-start(bf16[2,32,576]{2,1,0:T(8,128)(2,1)S(1)} %get-tuple-element.105), channel_id=1, source_target_pairs={{0,32},{4,36},{8,40},{12,44},{16,48},{20,52},{24,56},{28,60},{32,6... | collective-permute-start | bytes 221192 | tf_op jit(solution)/shard_map/ppermute | solution.py:56
  418.4 7.8 %collective-permute-start.39 = (bf16[2,32,576]{2,1,0:T(8,128)(2,1)S(1)}, bf16[2,32,576]{2,1,0:T(8,128)(2,1)S(1)}, u32[]{:S(2)}, u32[]{:S(2)}) collective-permute-start(bf16[2,32,576]{2,1,0:T(8,128)(2,1)S(1)} %get-tuple-element.107), channel_id=1, source_target_pairs={{0,32},{4,36},{8,40},{12,44},{16,48},{20,52},{24,56},{28,60},{32,6... | collective-permute-start | bytes 221192 | tf_op jit(solution)/shard_map/ppermute | solution.py:56
  420.3 6.0 %collective-permute-start.44 = (bf16[2,32,576]{2,1,0:T(8,128)(2,1)S(1)}, bf16[2,32,576]{2,1,0:T(8,128)(2,1)S(1)}, u32[]{:S(2)}, u32[]{:S(2)}) collective-permute-start(bf16[2,32,576]{2,1,0:T(8,128)(2,1)S(1)} %fusion.101), channel_id=1, source_target_pairs={{0,96},{4,100},{8,104},{12,108},{16,112},{20,116},{24,120},{28,124... | collective-permute-start | bytes 221192 | tf_op jit(solution)/shard_map/ppermute | solution.py:56
  424.2 10.0 %collective-permute-start.41 = (bf16[2,32,576]{2,1,0:T(8,128)(2,1)S(1)}, bf16[2,32,576]{2,1,0:T(8,128)(2,1)S(1)}, u32[]{:S(2)}, u32[]{:S(2)}) collective-permute-start(bf16[2,32,576]{2,1,0:T(8,128)(2,1)S(1)} %get-tuple-element.106), channel_id=1, source_target_pairs={{0,96},{4,100},{8,104},{12,108},{16,112},{20,116},{24,120},{28,124... | collective-permute-start | bytes 221192 | tf_op jit(solution)/shard_map/ppermute | solution.py:56
  426.3 5.7 %collective-permute-start.52 = (bf16[2,32,576]{2,1,0:T(8,128)(2,1)S(1)}, bf16[2,32,576]{2,1,0:T(8,128)(2,1)S(1)}, u32[]{:S(2)}, u32[]{:S(2)}) collective-permute-start(bf16[2,32,576]{2,1,0:T(8,128)(2,1)S(1)} %get-tuple-element.110), channel_id=1, source_target_pairs={{0,8},{4,12},{8,16},{12,20},{16,24},{20,28},{24,0},{28,4},{32,40},... | collective-permute-start | bytes 221192 | tf_op jit(solution)/shard_map/ppermute | solution.py:56
  426.3 8.0 %collective-permute-start.40 = (bf16[2,32,576]{2,1,0:T(8,128)(2,1)S(1)}, bf16[2,32,576]{2,1,0:T(8,128)(2,1)S(1)}, u32[]{:S(2)}, u32[]{:S(2)}) collective-permute-start(bf16[2,32,576]{2,1,0:T(8,128)(2,1)S(1)} %get-tuple-element.104), channel_id=1, source_target_pairs={{0,32},{4,36},{8,40},{12,44},{16,48},{20,52},{24,56},{28,60},{32,6... | collective-permute-start | bytes 221192 | tf_op jit(solution)/shard_map/ppermute | solution.py:56
  432.1 15.5 %collective-permute-start.59 = (bf16[16,576]{1,0:T(8,128)(2,1)S(1)}, bf16[16,576]{1,0:T(8,128)(2,1)S(1)}, u32[]{:S(2)}, u32[]{:S(2)}) collective-permute-start(bf16[16,576]{1,0:T(8,128)(2,1)S(1)} %slice_bitcast_fusion.79), channel_id=1, source_target_pairs={{0,96},{4,100},{8,104},{12,108},{16,112},{20,116},{24,120},{28,124... | collective-permute-start | bytes 55304 | tf_op jit(solution)/shard_map/ppermute | solution.py:56
  433.0 14.6 %collective-permute-start.60 = (bf16[16,576]{1,0:T(8,128)(2,1)S(1)}, bf16[16,576]{1,0:T(8,128)(2,1)S(1)}, u32[]{:S(2)}, u32[]{:S(2)}) collective-permute-start(bf16[16,576]{1,0:T(8,128)(2,1)S(1)} %slice_bitcast_fusion.77), channel_id=1, source_target_pairs={{0,32},{4,36},{8,40},{12,44},{16,48},{20,52},{24,56},{28,60},{32,6... | collective-permute-start | bytes 55304 | tf_op jit(solution)/shard_map/ppermute | solution.py:56
  444.3 5.5 collective-permute-start.62
  447.6 17.8 %collective-permute-start.24 = (bf16[256,1024]{1,0:T(8,128)(2,1)S(1)}, bf16[256,1024]{1,0:T(8,128)(2,1)S(1)}, u32[]{:S(2)}, u32[]{:S(2)}) collective-permute-start(bf16[256,1024]{1,0:T(8,128)(2,1)S(1)} %get-tuple-element.65), channel_id=1, source_target_pairs={{0,3},{1,0},{2,1},{3,2},{4,7},{5,4},{6,5},{7,6},{8,11},{9,8},{10,9... | collective-permute-start | bytes 1572872 | tf_op jit(solution)/shard_map/ppermute | solution.py:46
  454.2 31.4 %collective-permute-start.25 = (bf16[16,32,2048]{2,1,0:T(8,128)(2,1)S(1)}, bf16[16,32,2048]{2,1,0:T(8,128)(2,1)S(1)}, u32[]{:S(2)}, u32[]{:S(2)}) collective-permute-start(bf16[16,32,2048]{2,1,0:T(8,128)(2,1)S(1)} %dynamic-slice_bitcast_fusion), channel_id=1, source_target_pairs={{0,4},{4,0},{8,12},{12,8},{16,20},{20,16},{24,28},{28,24},{32,36},... | collective-permute-start | bytes 6291464 | tf_op jit(solution)/shard_map/ppermute | solution.py:56
  454.8 15.2 %collective-permute-start.10 = (bf16[256,1024]{1,0:T(8,128)(2,1)S(1)}, bf16[256,1024]{1,0:T(8,128)(2,1)S(1)}, u32[]{:S(2)}, u32[]{:S(2)}) collective-permute-start(bf16[256,1024]{1,0:T(8,128)(2,1)S(1)} %copy-done.48), channel_id=1, source_target_pairs={{0,1},{1,2},{2,3},{3,0},{4,5},{5,6},{6,7},{7,4},{8,9},{9,10},{10,1... | collective-permute-start | bytes 1572872 | tf_op jit(solution)/shard_map/ppermute | solution.py:46
  457.4 24.7 %collective-permute-start.12 = (bf16[256,1024]{1,0:T(8,128)(2,1)S(1)}, bf16[256,1024]{1,0:T(8,128)(2,1)S(1)}, u32[]{:S(2)}, u32[]{:S(2)}) collective-permute-start(bf16[256,1024]{1,0:T(8,128)(2,1)S(1)} %get-tuple-element.71), channel_id=1, source_target_pairs={{0,3},{1,0},{2,1},{3,2},{4,7},{5,4},{6,5},{7,6},{8,11},{9,8},{10,9... | collective-permute-start | bytes 1572872 | tf_op jit(solution)/shard_map/ppermute | solution.py:46
  486.8 6.4 %collective-permute-start.68 = (bf16[2,32,1024]{2,1,0:T(8,128)(2,1)S(1)}, bf16[2,32,1024]{2,1,0:T(8,128)(2,1)S(1)}, u32[]{:S(2)}, u32[]{:S(2)}) collective-permute-start(bf16[2,32,1024]{2,1,0:T(8,128)(2,1)S(1)} %get-tuple-element.90), channel_id=1, source_target_pairs={{0,24},{4,28},{8,0},{12,4},{16,8},{20,12},{24,16},{28,20},{32,56},... | collective-permute-start | bytes 393224 | tf_op jit(solution)/shard_map/ppermute | solution.py:56
  486.9 23.0 %collective-permute-start.66 = (bf16[2,32,1024]{2,1,0:T(8,128)(2,1)S(1)}, bf16[2,32,1024]{2,1,0:T(8,128)(2,1)S(1)}, u32[]{:S(2)}, u32[]{:S(2)}) collective-permute-start(bf16[2,32,1024]{2,1,0:T(8,128)(2,1)S(1)} %slice_bitcast_fusion.57), channel_id=1, source_target_pairs={{0,24},{4,28},{8,0},{12,4},{16,8},{20,12},{24,16},{28,20},{32,56},... | collective-permute-start | bytes 393224 | tf_op jit(solution)/shard_map/ppermute | solution.py:56
  487.2 12.3 %collective-permute-start.67 = (bf16[2,32,1024]{2,1,0:T(8,128)(2,1)S(1)}, bf16[2,32,1024]{2,1,0:T(8,128)(2,1)S(1)}, u32[]{:S(2)}, u32[]{:S(2)}) collective-permute-start(bf16[2,32,1024]{2,1,0:T(8,128)(2,1)S(1)} %get-tuple-element.88), channel_id=1, source_target_pairs={{0,8},{4,12},{8,16},{12,20},{16,24},{20,28},{24,0},{28,4},{32,40},... | collective-permute-start | bytes 393224 | tf_op jit(solution)/shard_map/ppermute | solution.py:56
  489.1 12.9 %collective-permute-start.64 = (bf16[2,32,1024]{2,1,0:T(8,128)(2,1)S(1)}, bf16[2,32,1024]{2,1,0:T(8,128)(2,1)S(1)}, u32[]{:S(2)}, u32[]{:S(2)}) collective-permute-start(bf16[2,32,1024]{2,1,0:T(8,128)(2,1)S(1)} %get-tuple-element.89), channel_id=1, source_target_pairs={{0,8},{4,12},{8,16},{12,20},{16,24},{20,28},{24,0},{28,4},{32,40},... | collective-permute-start | bytes 393224 | tf_op jit(solution)/shard_map/ppermute | solution.py:56
  491.1 14.6 %collective-permute-start.29 = (bf16[2,32,1024]{2,1,0:T(8,128)(2,1)S(1)}, bf16[2,32,1024]{2,1,0:T(8,128)(2,1)S(1)}, u32[]{:S(2)}, u32[]{:S(2)}) collective-permute-start(bf16[2,32,1024]{2,1,0:T(8,128)(2,1)S(1)} %get-tuple-element.93), channel_id=1, source_target_pairs={{0,32},{4,36},{8,40},{12,44},{16,48},{20,52},{24,56},{28,60},{32,6... | collective-permute-start | bytes 393224 | tf_op jit(solution)/shard_map/ppermute | solution.py:56
  499.5 16.8 %collective-permute-start.28 = (bf16[2,32,1024]{2,1,0:T(8,128)(2,1)S(1)}, bf16[2,32,1024]{2,1,0:T(8,128)(2,1)S(1)}, u32[]{:S(2)}, u32[]{:S(2)}) collective-permute-start(bf16[2,32,1024]{2,1,0:T(8,128)(2,1)S(1)} %get-tuple-element.94), channel_id=1, source_target_pairs={{0,96},{4,100},{8,104},{12,108},{16,112},{20,116},{24,120},{28,124... | collective-permute-start | bytes 393224 | tf_op jit(solution)/shard_map/ppermute | solution.py:56
  502.0 7.4 %collective-permute-start.26 = (bf16[2,32,1024]{2,1,0:T(8,128)(2,1)S(1)}, bf16[2,32,1024]{2,1,0:T(8,128)(2,1)S(1)}, u32[]{:S(2)}, u32[]{:S(2)}) collective-permute-start(bf16[2,32,1024]{2,1,0:T(8,128)(2,1)S(1)} %get-tuple-element.95), channel_id=1, source_target_pairs={{0,32},{4,36},{8,40},{12,44},{16,48},{20,52},{24,56},{28,60},{32,6... | collective-permute-start | bytes 393224 | tf_op jit(solution)/shard_map/ppermute | solution.py:56
  503.1 6.3 %collective-permute-start.31 = (bf16[2,32,1024]{2,1,0:T(8,128)(2,1)S(1)}, bf16[2,32,1024]{2,1,0:T(8,128)(2,1)S(1)}, u32[]{:S(2)}, u32[]{:S(2)}) collective-permute-start(bf16[2,32,1024]{2,1,0:T(8,128)(2,1)S(1)} %fusion.84), channel_id=1, source_target_pairs={{0,96},{4,100},{8,104},{12,108},{16,112},{20,116},{24,120},{28,124... | collective-permute-start | bytes 393224 | tf_op jit(solution)/shard_map/ppermute | solution.py:56
  505.6 6.2 %collective-permute-start.65 = (bf16[2,32,1024]{2,1,0:T(8,128)(2,1)S(1)}, bf16[2,32,1024]{2,1,0:T(8,128)(2,1)S(1)}, u32[]{:S(2)}, u32[]{:S(2)}) collective-permute-start(bf16[2,32,1024]{2,1,0:T(8,128)(2,1)S(1)} %get-tuple-element.87), channel_id=1, source_target_pairs={{0,8},{4,12},{8,16},{12,20},{16,24},{20,28},{24,0},{28,4},{32,40},... | collective-permute-start | bytes 393224 | tf_op jit(solution)/shard_map/ppermute | solution.py:56
  509.5 6.8 %collective-permute-start.27 = (bf16[2,32,1024]{2,1,0:T(8,128)(2,1)S(1)}, bf16[2,32,1024]{2,1,0:T(8,128)(2,1)S(1)}, u32[]{:S(2)}, u32[]{:S(2)}) collective-permute-start(bf16[2,32,1024]{2,1,0:T(8,128)(2,1)S(1)} %get-tuple-element.92), channel_id=1, source_target_pairs={{0,32},{4,36},{8,40},{12,44},{16,48},{20,52},{24,56},{28,60},{32,6... | collective-permute-start | bytes 393224 | tf_op jit(solution)/shard_map/ppermute | solution.py:56
  512.1 27.4 %collective-permute-start.72 = (bf16[16,1024]{1,0:T(8,128)(2,1)S(1)}, bf16[16,1024]{1,0:T(8,128)(2,1)S(1)}, u32[]{:S(2)}, u32[]{:S(2)}) collective-permute-start(bf16[16,1024]{1,0:T(8,128)(2,1)S(1)} %slice_bitcast_fusion.63), channel_id=1, source_target_pairs={{0,96},{4,100},{8,104},{12,108},{16,112},{20,116},{24,120},{28,124... | collective-permute-start | bytes 98312 | tf_op jit(solution)/shard_map/ppermute | solution.py:56
  513.1 5.6 collective-permute-start.70
  514.2 14.4 %collective-permute-start.74 = (bf16[16,1024]{1,0:T(8,128)(2,1)S(1)}, bf16[16,1024]{1,0:T(8,128)(2,1)S(1)}, u32[]{:S(2)}, u32[]{:S(2)}) collective-permute-start(bf16[16,1024]{1,0:T(8,128)(2,1)S(1)} %get-tuple-element.136), channel_id=1, source_target_pairs={{0,96},{4,100},{8,104},{12,108},{16,112},{20,116},{24,120},{28,124... | collective-permute-start | bytes 98312 | tf_op jit(solution)/shard_map/ppermute | solution.py:56
  516.6 15.4 %collective-permute-start.34 = (bf16[16,1024]{1,0:T(8,128)(2,1)S(1)}, bf16[16,1024]{1,0:T(8,128)(2,1)S(1)}, u32[]{:S(2)}, u32[]{:S(2)}) collective-permute-start(bf16[16,1024]{1,0:T(8,128)(2,1)S(1)} %slice_bitcast_fusion.71), channel_id=1, source_target_pairs={{0,24},{4,28},{8,0},{12,4},{16,8},{20,12},{24,16},{28,20},{32,56},... | collective-permute-start | bytes 98312 | tf_op jit(solution)/shard_map/ppermute | solution.py:56
  518.6 13.4 %collective-permute-start.35 = (bf16[16,1024]{1,0:T(8,128)(2,1)S(1)}, bf16[16,1024]{1,0:T(8,128)(2,1)S(1)}, u32[]{:S(2)}, u32[]{:S(2)}) collective-permute-start(bf16[16,1024]{1,0:T(8,128)(2,1)S(1)} %slice_bitcast_fusion.69), channel_id=1, source_target_pairs={{0,8},{4,12},{8,16},{12,20},{16,24},{20,28},{24,0},{28,4},{32,40},... | collective-permute-start | bytes 98312 | tf_op jit(solution)/shard_map/ppermute | solution.py:56
  518.7 5.8 %collective-permute-start.32 = (bf16[16,1024]{1,0:T(8,128)(2,1)S(1)}, bf16[16,1024]{1,0:T(8,128)(2,1)S(1)}, u32[]{:S(2)}, u32[]{:S(2)}) collective-permute-start(bf16[16,1024]{1,0:T(8,128)(2,1)S(1)} %get-tuple-element.139), channel_id=1, source_target_pairs={{0,8},{4,12},{8,16},{12,20},{16,24},{20,28},{24,0},{28,4},{32,40},... | collective-permute-start | bytes 98312 | tf_op jit(solution)/shard_map/ppermute | solution.py:56
  528.6 6.7 %collective-permute-start.37 = (bf16[16,1024]{1,0:T(8,128)(2,1)S(1)}, bf16[16,1024]{1,0:T(8,128)(2,1)S(1)}, u32[]{:S(2)}, u32[]{:S(2)}) collective-permute-start(bf16[16,1024]{1,0:T(8,128)(2,1)S(1)} %fusion.119), channel_id=1, source_target_pairs={{0,24},{4,28},{8,0},{12,4},{16,8},{20,12},{24,16},{28,20},{32,56},... | collective-permute-start | bytes 98312 | tf_op jit(solution)/shard_map/ppermute | solution.py:56
  531.9 7.6 %collective-permute-start.73 = (bf16[16,1024]{1,0:T(8,128)(2,1)S(1)}, bf16[16,1024]{1,0:T(8,128)(2,1)S(1)}, u32[]{:S(2)}, u32[]{:S(2)}) collective-permute-start(bf16[16,1024]{1,0:T(8,128)(2,1)S(1)} %slice_bitcast_fusion.61), channel_id=1, source_target_pairs={{0,32},{4,36},{8,40},{12,44},{16,48},{20,52},{24,56},{28,60},{32,6... | collective-permute-start | bytes 98312 | tf_op jit(solution)/shard_map/ppermute | solution.py:56
  532.0 7.5 %collective-permute-start.71 = (bf16[16,1024]{1,0:T(8,128)(2,1)S(1)}, bf16[16,1024]{1,0:T(8,128)(2,1)S(1)}, u32[]{:S(2)}, u32[]{:S(2)}) collective-permute-start(bf16[16,1024]{1,0:T(8,128)(2,1)S(1)} %fusion.117), channel_id=1, source_target_pairs={{0,32},{4,36},{8,40},{12,44},{16,48},{20,52},{24,56},{28,60},{32,6... | collective-permute-start | bytes 98312 | tf_op jit(solution)/shard_map/ppermute | solution.py:56
  533.7 5.9 %collective-permute-start.75 = (bf16[16,1024]{1,0:T(8,128)(2,1)S(1)}, bf16[16,1024]{1,0:T(8,128)(2,1)S(1)}, u32[]{:S(2)}, u32[]{:S(2)}) collective-permute-start(bf16[16,1024]{1,0:T(8,128)(2,1)S(1)} %fusion.115), channel_id=1, source_target_pairs={{0,96},{4,100},{8,104},{12,108},{16,112},{20,116},{24,120},{28,124... | collective-permute-start | bytes 98312 | tf_op jit(solution)/shard_map/ppermute | solution.py:56
  536.1 10.0 %all-to-all-start.1 = ((f32[4,8,1920]{2,1,0:T(8,128)}), f32[4,8,1920]{2,1,0:T(8,128)S(1)}, u32[]{:S(2)}, u32[]{:S(2)}) async-start(f32[4,8,1920]{2,1,0:T(8,128)} %fusion.91), calls=%async_computation.1 | async-start | bytes 491520 | tf_op jit(solution)/shard_map/all_to_all | solution.py:324
  (82 other events, 1100.0 us)
Sparse Core Ops, SparseCore 0:
  27.6 52.4 all-gather.1
